TPU v7x, 32 devices: a whole 2x2x4 slice. The times are simulated.
32 devices in a mesh: rep: 8 (over z, x), grp: 4 (over y, core).
Axes of the slice: x: 2, y: 2, z: 4, core: 2. Of those that a mesh axis runs over, the one named last changes fastest.
Arguments:
- tokens: bfloat16 [32768, 960], P(('rep', 'grp')), may hold values from -6 to 6
- segments: int32 [32, 1024], P(('rep', 'grp')), may hold values from 0 to 3, never falling along the last dimension, each value on 1 to 512 neighbouring positions
- norm_attn: bfloat16 [960], P('grp'), may hold values from 0.5 to 1.5
- w_query: bfloat16 [960, 960], P('grp'), may hold values from -0.1875 to 0.1875
- w_key: bfloat16 [960, 320], P('grp'), may hold values from -0.1875 to 0.1875
- w_value: bfloat16 [960, 320], P('grp'), may hold values from -0.1875 to 0.1875
- w_out: bfloat16 [960, 960], P('grp'), may hold values from -1 to 1
- norm_mlp: bfloat16 [960], P('grp'), may hold values from 0.5 to 1.5
- w_gate: bfloat16 [960, 2560], P('grp'), may hold values from -0.1875 to 0.1875
- w_up: bfloat16 [960, 2560], P('grp'), may hold values from -0.1875 to 0.1875
- w_down: bfloat16 [2560, 960], P('grp'), may hold values from -0.125 to 0.125
- cotangent: bfloat16 [32768, 960], P(('rep', 'grp')), may hold values from -6 to 6
Outputs:
- mixed: bfloat16 [32768, 960], P(('rep', 'grp'))
- grad_tokens: float32 [32768, 960], P(('rep', 'grp'))
- grad_norm_attn: float32 [960], P('grp')
- grad_w_query: float32 [960, 960], P('grp')
- grad_w_key: float32 [960, 320], P('grp')
- grad_w_value: float32 [960, 320], P('grp')
- grad_w_out: float32 [960, 960], P('grp')
- grad_norm_mlp: float32 [960], P('grp')
- grad_w_gate: float32 [960, 2560], P('grp')
- grad_w_up: float32 [960, 2560], P('grp')
- grad_w_down: float32 [2560, 960], P('grp')
Inputs may be any that keep to these rules, and one draw needn't show every extreme that they name: `segments`: each row numbers the documents of one sequence in order from 0, never falling, each document 1 to 512 tokens long.
All inputs are finite; a program needn't handle non-finite values.
Results may differ from a plain program's by a relative error of at most 0.013.
Values may be sent and summed in bfloat16 or wider, within the bound.
A program may use at most 320 MiB of HBM per device.

v0:
```python
import jax
import jax.numpy as jnp
from jax import lax
from jax.sharding import PartitionSpec as P

QH = 15
KVH = 5
HD = 64


EPS = 1e-05
ROPE_BASE = 100000.0


def positions_of(segment_row):
    length = segment_row.shape[0]
    places = jnp.arange(length, dtype=jnp.int32)
    begins = jnp.concatenate([jnp.ones((1,), dtype=jnp.bool_), segment_row[1:] != segment_row[:-1]])
    firsts = lax.cummax(jnp.where(begins, places, jnp.zeros_like(places)), axis=0)
    return places - firsts


def rope_tables(positions, head_size):
    halfway = head_size // 2
    inverse = ROPE_BASE ** (-(jnp.arange(halfway, dtype=jnp.float32) * 2.0 / head_size))
    angles = positions.astype(jnp.float32)[:, None] * inverse[None, :]
    return (jnp.cos(angles), jnp.sin(angles))


def rotate(values, cosine, sine):
    halfway = values.shape[-1] // 2
    first_half = values[..., :halfway]
    second_half = values[..., halfway:]
    cos_rows = cosine[:, None, :]
    sin_rows = sine[:, None, :]
    return jnp.concatenate(
        [
            first_half * cos_rows - second_half * sin_rows,
            second_half * cos_rows + first_half * sin_rows,
        ],
        axis=-1,
    )


def rms_scale(values):
    return lax.rsqrt(jnp.mean(values * values, axis=-1, keepdims=True) + EPS)


def matmul(left, right):
    return jnp.dot(left, right, preferred_element_type=jnp.float32)


def left_product(rows_in, rows_grad):
    return jnp.einsum("te,tf->ef", rows_in, rows_grad, preferred_element_type=jnp.float32)


def right_product(rows_grad, weight):
    return jnp.einsum("tf,ef->te", rows_grad, weight, preferred_element_type=jnp.float32)


def norm_back(values, scale, gain, grad_normed):
    grad_gain = jnp.sum(grad_normed * values * scale, axis=0)
    scaled = grad_normed * gain.astype(jnp.float32)
    grad_values = scale * (
        scaled - values * scale * scale * jnp.mean(scaled * values, axis=-1, keepdims=True)
    )
    return (grad_gain, grad_values)


def block_scores(query_block, keys, segment_row, offset, scale):
    block = query_block.shape[0]
    length = keys.shape[0]
    query_places = offset + jnp.arange(block, dtype=jnp.int32)
    key_places = jnp.arange(length, dtype=jnp.int32)
    query_segments = segment_row[offset : offset + block]
    scores = (
        jnp.einsum("qkgd,tkd->kgqt", query_block, keys, preferred_element_type=jnp.float32) * scale
    )
    allowed = (query_segments[:, None] == segment_row[None, :]) & (
        key_places[None, :] <= query_places[:, None]
    )
    return jnp.where(allowed, scores, -1e30)


def shards(
    tokens,
    segments,
    norm_attn,
    w_query,
    w_key,
    w_value,
    w_out,
    norm_mlp,
    w_gate,
    w_up,
    w_down,
    cotangent,
):
    gain_attn, query_full, key_full, value_full, out_full = (
        lax.all_gather(norm_attn, "grp", axis=0, tiled=True),
        lax.all_gather(w_query, "grp", axis=0, tiled=True),
        lax.all_gather(w_key, "grp", axis=0, tiled=True),
        lax.all_gather(w_value, "grp", axis=0, tiled=True),
        lax.all_gather(w_out, "grp", axis=0, tiled=True),
    )
    gain_mlp, gate_full, up_full, down_full = (
        lax.all_gather(norm_mlp, "grp", axis=0, tiled=True),
        lax.all_gather(w_gate, "grp", axis=0, tiled=True),
        lax.all_gather(w_up, "grp", axis=0, tiled=True),
        lax.all_gather(w_down, "grp", axis=0, tiled=True),
    )
    length = tokens.shape[0]
    groups = QH // KVH
    scale = HD ** (-0.5)
    block = min(512, length)
    segment_row = segments[0]
    cosine, sine = rope_tables(positions_of(segment_row), HD)
    inputs = tokens.astype(jnp.float32)
    scale_attn = rms_scale(inputs)
    normed_attn = (inputs * scale_attn * gain_attn.astype(jnp.float32)).astype(jnp.bfloat16)
    queries = rotate(matmul(normed_attn, query_full).reshape(length, QH, HD), cosine, sine).astype(
        jnp.bfloat16
    )
    keys = rotate(matmul(normed_attn, key_full).reshape(length, KVH, HD), cosine, sine).astype(
        jnp.bfloat16
    )
    values = matmul(normed_attn, value_full).astype(jnp.bfloat16).reshape(length, KVH, HD)
    query_blocks = queries.reshape(length, KVH, groups, HD)
    outputs = []
    log_totals = []
    for offset in range(0, length, block):
        query_block = query_blocks[offset : offset + block]
        scores = block_scores(query_block, keys, segment_row, offset, scale)
        row_peak = jnp.max(scores, axis=-1, keepdims=True)
        exponent = jnp.exp(scores - row_peak)
        totals = jnp.sum(exponent, axis=-1, keepdims=True)
        probability = (exponent / totals).astype(jnp.bfloat16)
        outputs.append(
            jnp.einsum("kgqt,tkd->qkgd", probability, values, preferred_element_type=jnp.float32)
        )
        log_totals.append(row_peak + jnp.log(totals))
    attended = jnp.concatenate(outputs, axis=0).reshape(length, QH * HD).astype(jnp.bfloat16)
    residual = inputs + matmul(attended, out_full)
    scale_mlp = rms_scale(residual)
    normed_mlp = (residual * scale_mlp * gain_mlp.astype(jnp.float32)).astype(jnp.bfloat16)
    gate = matmul(normed_mlp, gate_full)
    upward = matmul(normed_mlp, up_full)
    sigmoid_gate = jax.nn.sigmoid(gate)
    silu_gate = gate * sigmoid_gate
    hidden = (silu_gate * upward).astype(jnp.bfloat16)
    mixed = (residual + matmul(hidden, down_full)).astype(jnp.bfloat16)
    gain_mlp, gate_full, up_full, down_full = (
        lax.all_gather(norm_mlp, "grp", axis=0, tiled=True),
        lax.all_gather(w_gate, "grp", axis=0, tiled=True),
        lax.all_gather(w_up, "grp", axis=0, tiled=True),
        lax.all_gather(w_down, "grp", axis=0, tiled=True),
    )
    grad_down = left_product(hidden, cotangent)
    grad_hidden = right_product(cotangent, down_full)
    grad_gate = (grad_hidden * upward * sigmoid_gate * (1.0 + gate * (1.0 - sigmoid_gate))).astype(
        jnp.bfloat16
    )
    grad_upward = (grad_hidden * silu_gate).astype(jnp.bfloat16)
    grad_wgate = left_product(normed_mlp, grad_gate)
    grad_wup = left_product(normed_mlp, grad_upward)
    grad_normed_mlp = right_product(grad_gate, gate_full) + right_product(grad_upward, up_full)
    grad_gain_mlp, grad_residual_norm = norm_back(residual, scale_mlp, gain_mlp, grad_normed_mlp)
    grad_residual = cotangent.astype(jnp.float32) + grad_residual_norm
    shard_gain_mlp, shard_gate, shard_up, shard_down = (
        lax.psum_scatter(grad_gain_mlp, "grp", scatter_dimension=0, tiled=True),
        lax.psum_scatter(grad_wgate, "grp", scatter_dimension=0, tiled=True),
        lax.psum_scatter(grad_wup, "grp", scatter_dimension=0, tiled=True),
        lax.psum_scatter(grad_down, "grp", scatter_dimension=0, tiled=True),
    )
    gain_attn, query_full, key_full, value_full, out_full = (
        lax.all_gather(norm_attn, "grp", axis=0, tiled=True),
        lax.all_gather(w_query, "grp", axis=0, tiled=True),
        lax.all_gather(w_key, "grp", axis=0, tiled=True),
        lax.all_gather(w_value, "grp", axis=0, tiled=True),
        lax.all_gather(w_out, "grp", axis=0, tiled=True),
    )
    grad_attn = grad_residual.astype(jnp.bfloat16)
    grad_wout = left_product(attended, grad_attn)
    grad_attended = (
        right_product(grad_attn, out_full).astype(jnp.bfloat16).reshape(length, KVH, groups, HD)
    )
    grad_keys = jnp.zeros((length, KVH, HD), jnp.float32)
    grad_values = jnp.zeros((length, KVH, HD), jnp.float32)
    grad_query_blocks = []
    for index, offset in enumerate(range(0, length, block)):
        query_block = query_blocks[offset : offset + block]
        grad_block = grad_attended[offset : offset + block]
        scores = block_scores(query_block, keys, segment_row, offset, scale)
        probability = jnp.exp(scores - log_totals[index])
        prob_low = probability.astype(jnp.bfloat16)
        grad_prob = jnp.einsum(
            "qkgd,tkd->kgqt", grad_block, values, preferred_element_type=jnp.float32
        )
        inner = jnp.sum(probability * grad_prob, axis=-1, keepdims=True)
        grad_scores = (probability * (grad_prob - inner)).astype(jnp.bfloat16)
        grad_query_blocks.append(
            jnp.einsum("kgqt,tkd->qkgd", grad_scores, keys, preferred_element_type=jnp.float32)
            * scale
        )
        grad_keys = (
            grad_keys
            + jnp.einsum(
                "kgqt,qkgd->tkd", grad_scores, query_block, preferred_element_type=jnp.float32
            )
            * scale
        )
        grad_values = grad_values + jnp.einsum(
            "kgqt,qkgd->tkd", prob_low, grad_block, preferred_element_type=jnp.float32
        )
    grad_query_rot = jnp.concatenate(grad_query_blocks, axis=0).reshape(length, QH, HD)
    grad_queries = (
        rotate(grad_query_rot, cosine, -sine).reshape(length, QH * HD).astype(jnp.bfloat16)
    )
    grad_keys_low = rotate(grad_keys, cosine, -sine).reshape(length, KVH * HD).astype(jnp.bfloat16)
    grad_values_low = grad_values.reshape(length, KVH * HD).astype(jnp.bfloat16)
    grad_wquery = left_product(normed_attn, grad_queries)
    grad_wkey = left_product(normed_attn, grad_keys_low)
    grad_wvalue = left_product(normed_attn, grad_values_low)
    grad_normed_attn = (
        right_product(grad_queries, query_full)
        + right_product(grad_keys_low, key_full)
        + right_product(grad_values_low, value_full)
    )
    grad_gain_attn, grad_input_norm = norm_back(inputs, scale_attn, gain_attn, grad_normed_attn)
    grad_inputs = grad_residual + grad_input_norm
    shard_gain_attn, shard_query, shard_key, shard_value, shard_out = (
        lax.psum_scatter(grad_gain_attn, "grp", scatter_dimension=0, tiled=True),
        lax.psum_scatter(grad_wquery, "grp", scatter_dimension=0, tiled=True),
        lax.psum_scatter(grad_wkey, "grp", scatter_dimension=0, tiled=True),
        lax.psum_scatter(grad_wvalue, "grp", scatter_dimension=0, tiled=True),
        lax.psum_scatter(grad_wout, "grp", scatter_dimension=0, tiled=True),
    )
    (
        shard_gain_attn,
        shard_query,
        shard_key,
        shard_value,
        shard_out,
        shard_gain_mlp,
        shard_gate,
        shard_up,
        shard_down,
    ) = lax.psum(
        (
            shard_gain_attn,
            shard_query,
            shard_key,
            shard_value,
            shard_out,
            shard_gain_mlp,
            shard_gate,
            shard_up,
            shard_down,
        ),
        "rep",
    )
    return (
        mixed,
        grad_inputs,
        shard_gain_attn,
        shard_query,
        shard_key,
        shard_value,
        shard_out,
        shard_gain_mlp,
        shard_gate,
        shard_up,
        shard_down,
    )


def solution(mesh):
    in_specs = (
        P(("rep", "grp"), None),
        P(("rep", "grp"), None),
        P("grp"),
        P("grp", None),
        P("grp", None),
        P("grp", None),
        P("grp", None),
        P("grp"),
        P("grp", None),
        P("grp", None),
        P("grp", None),
        P(("rep", "grp"), None),
    )
    out_specs = (
        P(("rep", "grp"), None),
        P(("rep", "grp"), None),
        P("grp"),
        P("grp", None),
        P("grp", None),
        P("grp", None),
        P("grp", None),
        P("grp"),
        P("grp", None),
        P("grp", None),
        P("grp", None),
    )
    return jax.shard_map(shards, mesh=mesh, in_specs=in_specs, out_specs=out_specs, check_vma=False)
```

profile of v0, /device:TPU:0, one launch (start us, length us, event | category | flops | bytes accessed | tf_op | source)
XLA Modules:
  0.0 1095.5 jit_solution(16916941109058675358)
XLA Ops:
  12.6 8.3 all-reduce.7
  22.1 11.5 %all-gather.1 = bf16[4,240,320]{1,2,0:T(8,128)(2,1)S(1)} all-gather(bf16[1,240,320]{1,2,0:T(8,128)(2,1)S(1)} %bitcast.178), channel_id=1, replica_groups=mesh['rep'=8,'grp'=4] {'grp'}, dimensions={0}, use_global_device_ids=true | all-gather | bytes 768000 | tf_op jit(solution)/shard_map/all_gather | solution.py:102
  34.6 8.2 all-gather
  51.8 3.9 fusion.63
  56.7 13.1 %fusion.71 = (f32[5,3,512]{2,1,0:T(4,128)S(1)}, f32[5,3,512,1024]{2,3,1,0:T(8,128)}) fusion(bf16[512,5,3,64]{0,3,2,1:T(8,128)(2,1)S(1)} %bitcast.158, bf16[1024,5,32]{0,2,1:T(8,128)(2,1)S(1)} %copy-done.11, bf16[1024,5,32]{0,2,1:T(8,128)(2,1)S(1)} %get-tuple-element.41, pred[512,1024]{0,1:T(8,128)(4,1)S(1)} %get-tuple-element.47), kind=kOutput, calls=%fused_computation.123 | convolution fusion | flops 1031528960 | bytes 33650688 | tf_op jit(solution)/shard_map/qkgd,tkd->kgqt/dot_general | solution.py:77
  69.8 13.8 %fusion.7 = f32[5,3,512]{2,1,0:T(4,128)S(1)} fusion(f32[5,3,512,1024]{2,3,1,0:T(8,128)} %get-tuple-element.53, f32[5,3,512]{2,1,0:T(4,128)S(1)} %get-tuple-element.52), kind=kLoop, calls=%fused_computation.19 | loop fusion | flops 15720960 | bytes 31518720 | tf_op jit(solution)/shard_map/reduce_sum | solution.py:136
  83.6 13.4 %fusion.47 = bf16[512,5,3,64]{0,3,2,1:T(8,128)(2,1)S(1)} fusion(bf16[1024,5,64,1]{0,2,3,1:T(8,128)(2,1)S(1)} %bitcast.168, f32[5,3,512,1024]{2,3,1,0:T(8,128)} %get-tuple-element.53, f32[5,3,512]{2,1,0:T(4,128)S(1)} %fusion.7, f32[5,3,512]{2,1,0:T(4,128)S(1)} %get-tuple-element.52), kind=kOutput, calls=%fused_computation.83 | convolution fusion | flops 1030717440 | bytes 33157120 | tf_op jit(solution)/shard_map/kgqt,tkd->qkgd/dot_general | solution.py:139
  97.0 13.2 %fusion.72 = (f32[5,3,512]{2,1,0:T(4,128)S(1)}, f32[5,3,512,1024]{2,3,1,0:T(8,128)}) fusion(bf16[512,5,3,64]{0,3,2,1:T(8,128)(2,1)S(1)} %bitcast.156, bf16[1024,5,32]{0,2,1:T(8,128)(2,1)S(1)} %copy-done.11, bf16[1024,5,32]{0,2,1:T(8,128)(2,1)S(1)} %get-tuple-element.41, pred[512,1024]{0,1:T(8,128)(4,1)S(1)} %get-tuple-element.46), kind=kOutput, calls=%fused_computation.124 | convolution fusion | flops 1031528960 | bytes 33650688 | tf_op jit(solution)/shard_map/qkgd,tkd->kgqt/dot_general | solution.py:77
  110.3 13.6 %fusion.6 = f32[5,3,512]{2,1,0:T(4,128)S(1)} fusion(f32[5,3,512,1024]{2,3,1,0:T(8,128)} %get-tuple-element.55, f32[5,3,512]{2,1,0:T(4,128)S(1)} %get-tuple-element.54), kind=kLoop, calls=%fused_computation.18 | loop fusion | flops 15720960 | bytes 31518720 | tf_op jit(solution)/shard_map/reduce_sum | solution.py:136
  123.9 13.0 %fusion.46 = bf16[512,5,3,64]{0,3,2,1:T(8,128)(2,1)S(1)} fusion(bf16[1024,5,64,1]{0,2,3,1:T(8,128)(2,1)S(1)} %bitcast.169, f32[5,3,512,1024]{2,3,1,0:T(8,128)} %get-tuple-element.55, f32[5,3,512]{2,1,0:T(4,128)S(1)} %fusion.6, f32[5,3,512]{2,1,0:T(4,128)S(1)} %get-tuple-element.54), kind=kOutput, calls=%fused_computation.82 | convolution fusion | flops 1030717440 | bytes 33157120 | tf_op jit(solution)/shard_map/kgqt,tkd->qkgd/dot_general | solution.py:139
  138.5 4.6 multiply_reduce_fusion.2
  146.7 10.9 fusion.74
  157.6 10.5 fusion.73
  168.1 13.3 %all-gather.16.cloned.1.call-done = bf16[2560,960]{0,1:T(8,128)(2,1)} async-done(((bf16[640,960]{0,1:T(8,128)(2,1)}), bf16[2560,960]{0,1:T(8,128)(2,1)}) %all-gather.16.cloned.1.call-update) | async-done | bytes 4915216 | tf_op jit(solution)/shard_map/all_gather | solution.py:110
  181.4 20.1 %multiply_convert_fusion = (bf16[1024,2560]{1,0:T(8,128)(2,1)}, bf16[1024,2560]{1,0:T(8,128)(2,1)}, bf16[1024,2560]{1,0:T(8,128)(2,1)}) fusion(f32[1024,2560]{1,0:T(8,128)} %fusion.73, f32[1024,2560]{1,0:T(8,128)} %fusion.74, bf16[1024,960]{0,1:T(8,128)(2,1)} %param.23, bf16[2560,960]{0,1:T(8,128)(2,1)} %all-gather.16.cloned.1.call-done), kind=kOutput, calls=%fused_computation.28 | convolution fusion | flops 5072486400 | bytes 43581440 | tf_op jit(solution)/shard_map/tf,ef->te/dot_general | solution.py:58
  201.5 9.3 fusion.75
  210.8 9.0 multiply_reduce_fusion
  221.4 2.2 convolution_convert_fusion
  223.8 13.6 %fusion.34 = f32[5,64,1024]{2,1,0:T(8,128)} fusion(bf16[512,5,3,64]{0,3,2,1:T(8,128)(2,1)S(1)} %bitcast.160, f32[5,3,512,1024]{2,3,1,0:T(8,128)} %get-tuple-element.55, f32[5,3,512]{2,1,0:T(4,128)S(1)} %log_add_fusion.1), kind=kOutput, calls=%fused_computation.75 | convolution fusion | flops 1022361600 | bytes 33781760 | tf_op jit(solution)/shard_map/kgqt,qkgd->tkd/dot_general | solution.py:212
  237.3 23.8 %fusion.3 = (f32[5,3,512]{2,1,0:T(4,128)S(1)}, f32[5,1024,512,3]{2,1,3,0:T(8,128)}) fusion(f32[5,3,512,1024]{2,3,1,0:T(8,128)} %get-tuple-element.55, f32[5,3,512]{2,1,0:T(4,128)S(1)} %log_add_fusion.1, bf16[1024,5,64,1]{0,2,3,1:T(8,128)(2,1)} %bitcast.167, bf16[512,5,3,64]{0,3,2,1:T(8,128)(2,1)S(1)} %bitcast.161), kind=kOutput, calls=%fused_computation.7 | convolution fusion | flops 1030218240 | bytes 64614400 | tf_op jit(solution)/shard_map/qkgd,tkd->kgqt/dot_general | solution.py:196
  261.2 23.8 %fusion = (f32[5,3,512]{2,1,0:T(4,128)S(1)}, f32[5,1024,512,3]{2,1,3,0:T(8,128)}) fusion(f32[5,3,512,1024]{2,3,1,0:T(8,128)} %get-tuple-element.53, f32[5,3,512]{2,1,0:T(4,128)S(1)} %log_add_fusion, bf16[1024,5,64,1]{0,2,3,1:T(8,128)(2,1)S(1)} %bitcast.170, bf16[512,5,3,64]{0,3,2,1:T(8,128)(2,1)S(1)} %bitcast.162), kind=kOutput, calls=%fused_computation.2 | convolution fusion | flops 1030218240 | bytes 64614400 | tf_op jit(solution)/shard_map/qkgd,tkd->kgqt/dot_general | solution.py:196
  285.0 13.6 %fusion.43 = bf16[5,64,1024]{2,1,0:T(8,128)(2,1)} fusion(f32[5,64,1024]{2,1,0:T(8,128)S(1)} %copy-done.13, bf16[512,5,3,64]{0,3,2,1:T(8,128)(2,1)S(1)} %bitcast.163, f32[5,3,512,1024]{2,3,1,0:T(8,128)} %get-tuple-element.53, f32[5,3,512]{2,1,0:T(4,128)S(1)} %log_add_fusion), kind=kOutput, calls=%fused_computation.80 | convolution fusion | flops 1023016960 | bytes 34437120 | tf_op jit(solution)/shard_map/kgqt,qkgd->tkd/dot_general | solution.py:212
  298.6 3.4 fusion.57
  302.2 27.2 %fusion.2 = bf16[5,3,512,1024]{2,3,1,0:T(8,128)(2,1)} fusion(f32[5,1024,512,3]{2,1,3,0:T(8,128)} %get-tuple-element.60, f32[5,3,512,1024]{2,3,1,0:T(8,128)} %get-tuple-element.53, f32[5,3,512]{2,1,0:T(4,128)S(1)} %get-tuple-element.59, f32[5,3,512]{2,1,0:T(4,128)S(1)} %log_add_fusion), kind=kLoop, calls=%fused_computation.4 | loop fusion | flops 31457280 | bytes 78704640 | tf_op jit(solution)/shard_map/convert_element_type | solution.py:200
  329.4 26.7 %fusion.5 = bf16[5,3,512,1024]{2,3,1,0:T(8,128)(2,1)} fusion(f32[5,1024,512,3]{2,1,3,0:T(8,128)} %get-tuple-element.62, f32[5,3,512,1024]{2,3,1,0:T(8,128)} %get-tuple-element.55, f32[5,3,512]{2,1,0:T(4,128)S(1)} %get-tuple-element.61, f32[5,3,512]{2,1,0:T(4,128)S(1)} %log_add_fusion.1), kind=kLoop, calls=%fused_computation.9 | loop fusion | flops 31457280 | bytes 78704640 | tf_op jit(solution)/shard_map/convert_element_type | solution.py:200
  356.0 10.4 convolution_bitcast_fusion
  366.4 11.4 %fusion.50 = f32[1024,5,64]{0,2,1:T(8,128)} fusion(f32[5,64,1024]{2,1,0:T(8,128)S(1)} %convolution_bitcast_fusion, bf16[512,5,3,64]{0,3,2,1:T(8,128)(2,1)S(1)} %bitcast.157, bf16[5,3,512,1024]{2,3,1,0:T(8,128)(2,1)} %fusion.5), kind=kOutput, calls=%fused_computation.86 | convolution fusion | flops 1007288320 | bytes 19333120 | tf_op jit(solution)/shard_map/kgqt,qkgd->tkd/dot_general | solution.py:207
  379.4 2.3 fusion.59
  381.8 6.8 fusion.52
  389.8 8.4 multiply_bitcast_fusion
  398.2 8.3 multiply_bitcast_fusion.1
  409.0 4.1 fusion.61
  413.2 10.5 fusion.80
  423.8 10.4 fusion.78
  434.2 10.5 fusion.77
  448.8 6.2 reduce-scatter.14.cloned.1.call-done
  454.9 45.6 %reduce-scatter.12.cloned.1.call-done = f32[240,960]{1,0:T(8,128)} async-done(((f32[960,960]{1,0:T(8,128)}), f32[240,960]{1,0:T(8,128)}) %reduce-scatter.12.cloned.1.call-update) | async-done | bytes 921616 | tf_op jit(solution)/shard_map/reduce_scatter | solution.py:233
  500.6 83.5 %reduce-scatter.20.cloned.1.call-done = f32[640,960]{0,1:T(8,128)} async-done(((f32[2560,960]{0,1:T(8,128)}), f32[640,960]{0,1:T(8,128)}) %reduce-scatter.20.cloned.1.call-update) | async-done | bytes 2457616 | tf_op jit(solution)/shard_map/reduce_scatter | solution.py:173
  584.1 83.7 %reduce-scatter.18.cloned.1.call-done = f32[240,2560]{1,0:T(8,128)} async-done(((f32[960,2560]{1,0:T(8,128)}), f32[240,2560]{1,0:T(8,128)}) %reduce-scatter.18.cloned.1.call-update) | async-done | bytes 2457616 | tf_op jit(solution)/shard_map/reduce_scatter | solution.py:172
  667.7 83.5 %reduce-scatter.16.cloned.1.call-done = f32[240,2560]{1,0:T(8,128)} async-done(((f32[960,2560]{1,0:T(8,128)}), f32[240,2560]{1,0:T(8,128)}) %reduce-scatter.16.cloned.1.call-update) | async-done | bytes 2457616 | tf_op jit(solution)/shard_map/reduce_scatter | solution.py:171
  756.8 3.9 fusion.29
  760.6 5.8 all-reduce.6
  766.6 23.2 %all-reduce.4 = (f32[240]{0:T(256)}, f32[240]{0:T(256)}) all-reduce(f32[240]{0:T(256)S(1)} %dynamic-slice.3, f32[240]{0:T(256)S(1)} %dynamic-slice.5), channel_id=1, replica_groups=mesh['rep'=8,'grp'=4] {'rep'}, use_global_device_ids=true, to_apply=%region_14.15 | all-reduce | flops 480 | bytes 3840 | tf_op jit(solution)/shard_map/psum | solution.py:248
  789.9 6.6 fusion.25
  796.4 9.7 add_convert_fusion
  806.1 269.7 %all-reduce.10.cloned.1.call-done = (f32[240,960]{1,0:T(8,128)}, f32[240,320]{0,1:T(8,128)}, f32[240,320]{0,1:T(8,128)}, f32[240,960]{1,0:T(8,128)}, f32[240,256...) async-done(((f32[240,960]{1,0:T(8,128)}, f32[240,320]{0,1:T(8,128)}, f32[240,320]{0,1:T(8,128)}, f32[240,960]{1,0:T(8,128)}, f32[240,2560]{1,0:T(8,128)}, ...) | async-done | bytes 9830416 | tf_op jit(solution)/shard_map/psum | solution.py:248
  1075.9 2.4 copy.78
  1081.9 2.2 copy.81
  (179 shorter events, 45.8 us)
Async XLA Ops:
  7.2 3.7 copy-start.40
  7.2 3.5 copy-start.34
  7.2 4.9 copy-start.43
  7.2 5.2 copy-start.44
  7.2 14.4 %copy-start = (bf16[1024,960]{0,1:T(8,128)(2,1)S(1)}, bf16[1024,960]{0,1:T(8,128)(2,1)}, u32[]{:S(2)}) copy-start(bf16[1024,960]{0,1:T(8,128)(2,1)} %param.12) | copy-start | bytes 5898244
  7.2 14.9 %copy-start.32 = (bf16[240,320]{0,1:T(8,128)(2,1)S(1)}, bf16[240,320]{0,1:T(8,128)(2,1)}, u32[]{:S(2)}) copy-start(bf16[240,320]{0,1:T(8,128)(2,1)} %param.16) | copy-start | bytes 460804
  7.2 44.5 %all-gather.8.cloned.1.call-start = ((), (), s32[]{:S(2)}) async-start(), calls=%async_computation.7 | async-start | bytes 2457600 | tf_op jit(solution)/shard_map/all_gather | solution.py:101
  8.0 130.5 %all-gather.10.cloned.1.call-start = ((), (), s32[]{:S(2)}) async-start(), calls=%async_computation.8 | async-start | bytes 2457600 | tf_op jit(solution)/shard_map/all_gather | solution.py:104
  8.7 138.0 %all-gather.14.cloned.1.call-start = ((), (), s32[]{:S(2)}) async-start(), calls=%async_computation.10 | async-start | bytes 6144000 | tf_op jit(solution)/shard_map/all_gather | solution.py:109
  9.5 25.2 %copy-start.33 = (bf16[240,320]{0,1:T(8,128)(2,1)S(1)}, bf16[240,320]{0,1:T(8,128)(2,1)}, u32[]{:S(2)}) copy-start(bf16[240,320]{0,1:T(8,128)(2,1)} %param.17) | copy-start | bytes 460804
  9.5 148.1 %all-gather.12.cloned.1.call-start = ((), (), s32[]{:S(2)}) async-start(), calls=%async_computation.9 | async-start | bytes 6144000 | tf_op jit(solution)/shard_map/all_gather | solution.py:108
  10.0 171.3 %all-gather.16.cloned.1.call-start = ((), (), s32[]{:S(2)}) async-start(), calls=%async_computation.11 | async-start | bytes 6144000 | tf_op jit(solution)/shard_map/all_gather | solution.py:110
  10.6 434.4 %reduce-scatter.24.cloned.1.call-start = ((), (), s32[]{:S(2)}) async-start(), calls=%async_computation.18 | async-start | bytes 1843200
  20.9 30.8 %copy-start.35 = (f32[960]{0:T(1024)}, f32[960]{0:T(1024)S(1)}, u32[]{:S(2)}) copy-start(f32[960]{0:T(1024)S(1)} %convert_element_type.90) | copy-start | bytes 11524
  22.1 29.7 %copy-start.37 = (f32[1024]{0:T(1024)}, f32[1024]{0:T(1024)S(1)}, u32[]{:S(2)}) copy-start(f32[1024]{0:T(1024)S(1)} %add_rsqrt_fusion.1) | copy-start | bytes 12292
  34.6 13.3 %copy-start.20 = (bf16[960,320]{0,1:T(8,128)(2,1)}, bf16[960,320]{0,1:T(8,128)(2,1)S(1)}, u32[]{:S(2)}) copy-start(bf16[960,320]{0,1:T(8,128)(2,1)S(1)} %reshape.228) | copy-start | bytes 1843204
  46.2 2.7 copy-start.18
  50.1 5.6 copy-start.14
  51.0 46.0 %copy-start.9 = (bf16[1024,5,32]{0,2,1:T(8,128)(2,1)}, bf16[1024,5,32]{0,2,1:T(8,128)(2,1)S(1)}, u32[]{:S(2)}) copy-start(bf16[1024,5,32]{0,2,1:T(8,128)(2,1)S(1)} %get-tuple-element.41) | copy-start | bytes 983044
  51.8 4.0 copy-start.31
  56.6 13.2 %copy-start.7 = (bf16[512,15,64]{0,2,1:T(8,128)(2,1)}, bf16[512,15,64]{0,2,1:T(8,128)(2,1)S(1)}, u32[]{:S(2)}) copy-start(bf16[512,15,64]{0,2,1:T(8,128)(2,1)S(1)} %get-tuple-element.38) | copy-start | bytes 2949124
  56.6 40.4 %copy-start.5 = (bf16[512,15,64]{0,2,1:T(8,128)(2,1)}, bf16[512,15,64]{0,2,1:T(8,128)(2,1)S(1)}, u32[]{:S(2)}) copy-start(bf16[512,15,64]{0,2,1:T(8,128)(2,1)S(1)} %get-tuple-element.37) | copy-start | bytes 2949124
  69.8 13.8 %copy-start.16 = (bf16[1024,320]{0,1:T(8,128)(2,1)S(1)}, bf16[1024,320]{0,1:T(8,128)(2,1)}, u32[]{:S(2)}) copy-start(bf16[1024,320]{0,1:T(8,128)(2,1)} %convolution_convert_fusion.1) | copy-start | bytes 1966084
  201.5 9.3 copy-start.2
  201.5 9.3 copy-start.45
  210.8 9.1 copy-start.26
  221.4 2.2 copy-start.4
  237.3 23.9 %copy-start.17 = (bf16[1024,320]{0,1:T(8,128)(2,1)S(1)}, bf16[1024,320]{0,1:T(8,128)(2,1)}, u32[]{:S(2)}) copy-start(bf16[1024,320]{0,1:T(8,128)(2,1)} %convolution_convert_fusion.1) | copy-start | bytes 1966084
  261.2 23.8 %copy-start.13 = (f32[5,64,1024]{2,1,0:T(8,128)S(1)}, f32[5,64,1024]{2,1,0:T(8,128)}, u32[]{:S(2)}) copy-start(f32[5,64,1024]{2,1,0:T(8,128)} %fusion.34) | copy-start | bytes 3932164
  285.0 13.6 %copy-start.36 = (f32[960]{0:T(1024)S(1)}, f32[960]{0:T(1024)}, u32[]{:S(2)}) copy-start(f32[960]{0:T(1024)} %copy-done.35) | copy-start | bytes 11524
  285.0 13.6 %copy-start.38 = (f32[1024]{0:T(1024)S(1)}, f32[1024]{0:T(1024)}, u32[]{:S(2)}) copy-start(f32[1024]{0:T(1024)} %copy-done.37) | copy-start | bytes 12292
  302.1 144.8 %reduce-scatter.22.cloned.1.call-start = ((), (), s32[]{:S(2)}) async-start(), calls=%async_computation.17 | async-start | bytes 1843200
  329.4 26.7 %copy-start.8 = (bf16[512,15,64]{0,2,1:T(8,128)(2,1)S(1)}, bf16[512,15,64]{0,2,1:T(8,128)(2,1)}, u32[]{:S(2)}) copy-start(bf16[512,15,64]{0,2,1:T(8,128)(2,1)} %copy-done.7) | copy-start | bytes 2949124
  356.0 10.4 copy-start.6
  366.4 11.4 %copy-start.15 = (f32[1024,32]{0,1:T(8,128)S(1)}, f32[1024,32]{0,1:T(8,128)}, u32[]{:S(2)}) copy-start(f32[1024,32]{0,1:T(8,128)} %copy-done.14) | copy-start | bytes 393220
  366.4 11.4 %copy-start.29 = (f32[1024,32]{0,1:T(8,128)S(1)}, f32[1024,32]{0,1:T(8,128)}, u32[]{:S(2)}) copy-start(f32[1024,32]{0,1:T(8,128)} %get-tuple-element.43) | copy-start | bytes 393220
  381.8 73.2 %reduce-scatter.14.cloned.1.call-start = ((), (), s32[]{:S(2)}) async-start(), calls=%async_computation.13 | async-start | bytes 4915200 | tf_op jit(solution)/shard_map/reduce_scatter | solution.py:236
  388.6 111.9 %reduce-scatter.12.cloned.1.call-start = ((), (), s32[]{:S(2)}) async-start(), calls=%async_computation.12 | async-start | bytes 4915200 | tf_op jit(solution)/shard_map/reduce_scatter | solution.py:233
  413.2 170.9 %reduce-scatter.20.cloned.1.call-start = ((), (), s32[]{:S(2)}) async-start(), calls=%async_computation.16 | async-start | bytes 12288000 | tf_op jit(solution)/shard_map/reduce_scatter | solution.py:173
  423.7 244.0 %reduce-scatter.18.cloned.1.call-start = ((), (), s32[]{:S(2)}) async-start(), calls=%async_computation.15 | async-start | bytes 12288000 | tf_op jit(solution)/shard_map/reduce_scatter | solution.py:172
  434.2 317.1 %reduce-scatter.16.cloned.1.call-start = ((), (), s32[]{:S(2)}) async-start(), calls=%async_computation.14 | async-start | bytes 12288000 | tf_op jit(solution)/shard_map/reduce_scatter | solution.py:171
  444.7 631.2 %all-reduce.10.cloned.1.call-start = ((), (), s32[]{:S(2)}) async-start(), calls=%async_computation.19 | async-start | bytes 19988480 | tf_op jit(solution)/shard_map/psum | solution.py:248
  754.5 2.2 copy-start.22
  756.8 3.9 copy-start.39
  789.9 6.6 copy-start.3
  1075.9 8.2 copy-start.25
  1078.3 7.3 copy-start.24
  1084.1 3.0 copy-start.23
  (11 other events, 15.9 us)
Sparse Core Ops, SparseCore 0:
  9.6 28.0 all-gather.7
  39.3 21.8 all-gather.9
  62.8 38.5 all-gather.13
  102.8 38.5 all-gather.11
  142.8 38.5 all-gather.15
  302.2 27.5 reduce-scatter.23
  381.9 27.5 reduce-scatter.21
  412.0 42.9 reduce-scatter.13
  457.6 42.8 reduce-scatter.11
  503.0 80.9 reduce-scatter.19
  586.7 81.0 reduce-scatter.17
  670.2 81.0 reduce-scatter.15
  757.4 318.3 all-reduce.9
where the time goes:
time: 1100 us
  waiting for transfers between devices  589 us (54%)
  matrix products  304 us (28%)
  other arithmetic  99.6 us (9%)
  blocking collectives  57.1 us (5%)
  local copies, waits for them, and re-layouts  28.3 us (3%)
  between operations  16.4 us (1%)
    psum x1, waiting for transfers between devices, shards(): lax.psum((shard_gain_attn, shard_query, shard_key, shard_value, shard_out...  270 us
    reduce_scatter x1, waiting for transfers between devices, shards(): lax.psum_scatter(grad_wup, 'grp', scatter_dimension=0, tiled=True)  83.7 us
    reduce_scatter x1, waiting for transfers between devices, shards(): lax.psum_scatter(grad_wgate, 'grp', scatter_dimension=0, tiled=True)  83.5 us
    reduce_scatter x1, waiting for transfers between devices, shards(): lax.psum_scatter(grad_down, 'grp', scatter_dimension=0, tiled=True)  83.5 us
    convert_element_type x2, other arithmetic, shards(): grad_scores = (probability * (grad_prob - inner)).astype(jnp.bfloat16)  53.9 us
    dot_general x7, matrix products, right_product(): jnp.einsum('tf,ef->te', rows_grad, weight, preferred_element_type=jnp.flo...  47.9 us
    dot_general x2, matrix products, shards(): jnp.einsum('qkgd,tkd->kgqt', grad_block, values, preferred_element_type=j...  47.7 us
    reduce_scatter x1, waiting for transfers between devices, shards(): lax.psum_scatter(grad_wquery, 'grp', scatter_dimension=0, tiled=True)  45.6 us
  transfers between devices with their start and end apart: 13, of which 7 were waited for; matrix products, arithmetic and copies ran while one was open for 27% of the time, Pallas kernels for 0%

commit v1 on v0

--- a/solution.py
+++ b/solution.py
@@ -96,19 +96,30 @@
     w_down,
     cotangent,
 ):
-    gain_attn, query_full, key_full, value_full, out_full = (
-        lax.all_gather(norm_attn, "grp", axis=0, tiled=True),
-        lax.all_gather(w_query, "grp", axis=0, tiled=True),
-        lax.all_gather(w_key, "grp", axis=0, tiled=True),
-        lax.all_gather(w_value, "grp", axis=0, tiled=True),
-        lax.all_gather(w_out, "grp", axis=0, tiled=True),
-    )
-    gain_mlp, gate_full, up_full, down_full = (
-        lax.all_gather(norm_mlp, "grp", axis=0, tiled=True),
-        lax.all_gather(w_gate, "grp", axis=0, tiled=True),
-        lax.all_gather(w_up, "grp", axis=0, tiled=True),
-        lax.all_gather(w_down, "grp", axis=0, tiled=True),
-    )
+    dim = tokens.shape[1]
+    kv = w_key.shape[1]
+    ff = w_gate.shape[1]
+    rows = w_query.shape[0]
+    pack_attn = jnp.concatenate(
+        [
+            w_query,
+            w_key,
+            w_value,
+            w_out,
+            jnp.pad(jnp.stack([norm_attn, norm_mlp], axis=1), ((0, 0), (0, 126))),
+        ],
+        axis=1,
+    )
+    full_attn = lax.all_gather(pack_attn, "grp", axis=0, tiled=True)
+    query_full = full_attn[:, :dim]
+    key_full = full_attn[:, dim : dim + kv]
+    value_full = full_attn[:, dim + kv : dim + 2 * kv]
+    out_full = full_attn[:, dim + 2 * kv : 2 * dim + 2 * kv]
+    gain_attn = full_attn[:, 2 * dim + 2 * kv]
+    gain_mlp = full_attn[:, 2 * dim + 2 * kv + 1]
+    gate_full = lax.all_gather(w_gate, "grp", axis=0, tiled=True)
+    up_full = lax.all_gather(w_up, "grp", axis=0, tiled=True)
+    down_full = lax.all_gather(w_down, "grp", axis=0, tiled=True)
     length = tokens.shape[0]
     groups = QH // KVH
     scale = HD ** (-0.5)
@@ -149,12 +160,6 @@
     silu_gate = gate * sigmoid_gate
     hidden = (silu_gate * upward).astype(jnp.bfloat16)
     mixed = (residual + matmul(hidden, down_full)).astype(jnp.bfloat16)
-    gain_mlp, gate_full, up_full, down_full = (
-        lax.all_gather(norm_mlp, "grp", axis=0, tiled=True),
-        lax.all_gather(w_gate, "grp", axis=0, tiled=True),
-        lax.all_gather(w_up, "grp", axis=0, tiled=True),
-        lax.all_gather(w_down, "grp", axis=0, tiled=True),
-    )
     grad_down = left_product(hidden, cotangent)
     grad_hidden = right_product(cotangent, down_full)
     grad_gate = (grad_hidden * upward * sigmoid_gate * (1.0 + gate * (1.0 - sigmoid_gate))).astype(
@@ -166,19 +171,14 @@
     grad_normed_mlp = right_product(grad_gate, gate_full) + right_product(grad_upward, up_full)
     grad_gain_mlp, grad_residual_norm = norm_back(residual, scale_mlp, gain_mlp, grad_normed_mlp)
     grad_residual = cotangent.astype(jnp.float32) + grad_residual_norm
-    shard_gain_mlp, shard_gate, shard_up, shard_down = (
-        lax.psum_scatter(grad_gain_mlp, "grp", scatter_dimension=0, tiled=True),
-        lax.psum_scatter(grad_wgate, "grp", scatter_dimension=0, tiled=True),
-        lax.psum_scatter(grad_wup, "grp", scatter_dimension=0, tiled=True),
-        lax.psum_scatter(grad_down, "grp", scatter_dimension=0, tiled=True),
-    )
-    gain_attn, query_full, key_full, value_full, out_full = (
-        lax.all_gather(norm_attn, "grp", axis=0, tiled=True),
-        lax.all_gather(w_query, "grp", axis=0, tiled=True),
-        lax.all_gather(w_key, "grp", axis=0, tiled=True),
-        lax.all_gather(w_value, "grp", axis=0, tiled=True),
-        lax.all_gather(w_out, "grp", axis=0, tiled=True),
-    )
+    grad_gu = jnp.concatenate([grad_wgate, grad_wup], axis=1).astype(jnp.bfloat16)
+    grad_down = grad_down.astype(jnp.bfloat16)
+    grad_gu, grad_down, grad_residual = lax.optimization_barrier(
+        (grad_gu, grad_down, grad_residual)
+    )
+    shard_gu = lax.psum_scatter(grad_gu, "grp", scatter_dimension=0, tiled=True)
+    shard_down = lax.psum_scatter(grad_down, "grp", scatter_dimension=0, tiled=True)
+    shard_gu, shard_down = lax.psum((shard_gu, shard_down), "rep")
     grad_attn = grad_residual.astype(jnp.bfloat16)
     grad_wout = left_product(attended, grad_attn)
     grad_attended = (
@@ -228,37 +228,28 @@
     )
     grad_gain_attn, grad_input_norm = norm_back(inputs, scale_attn, gain_attn, grad_normed_attn)
     grad_inputs = grad_residual + grad_input_norm
-    shard_gain_attn, shard_query, shard_key, shard_value, shard_out = (
-        lax.psum_scatter(grad_gain_attn, "grp", scatter_dimension=0, tiled=True),
-        lax.psum_scatter(grad_wquery, "grp", scatter_dimension=0, tiled=True),
-        lax.psum_scatter(grad_wkey, "grp", scatter_dimension=0, tiled=True),
-        lax.psum_scatter(grad_wvalue, "grp", scatter_dimension=0, tiled=True),
-        lax.psum_scatter(grad_wout, "grp", scatter_dimension=0, tiled=True),
-    )
-    (
-        shard_gain_attn,
-        shard_query,
-        shard_key,
-        shard_value,
-        shard_out,
-        shard_gain_mlp,
-        shard_gate,
-        shard_up,
-        shard_down,
-    ) = lax.psum(
-        (
-            shard_gain_attn,
-            shard_query,
-            shard_key,
-            shard_value,
-            shard_out,
-            shard_gain_mlp,
-            shard_gate,
-            shard_up,
-            shard_down,
-        ),
-        "rep",
-    )
+    pack_grad = jnp.concatenate(
+        [
+            grad_wquery,
+            grad_wkey,
+            grad_wvalue,
+            grad_wout,
+            jnp.pad(jnp.stack([grad_gain_attn, grad_gain_mlp], axis=1), ((0, 0), (0, 126))),
+        ],
+        axis=1,
+    ).astype(jnp.bfloat16)
+    shard_attn = lax.psum_scatter(pack_grad, "grp", scatter_dimension=0, tiled=True)
+    shard_attn, shard_gu, shard_down = lax.optimization_barrier((shard_attn, shard_gu, shard_down))
+    shard_attn = lax.psum(shard_attn, "rep").astype(jnp.float32)
+    shard_query = shard_attn[:, :dim]
+    shard_key = shard_attn[:, dim : dim + kv]
+    shard_value = shard_attn[:, dim + kv : dim + 2 * kv]
+    shard_out = shard_attn[:, dim + 2 * kv : 2 * dim + 2 * kv]
+    shard_gain_attn = shard_attn[:, 2 * dim + 2 * kv]
+    shard_gain_mlp = shard_attn[:, 2 * dim + 2 * kv + 1]
+    shard_gate = shard_gu[:, :ff].astype(jnp.float32)
+    shard_up = shard_gu[:, ff:].astype(jnp.float32)
+    shard_down = shard_down.astype(jnp.float32)
     return (
         mixed,
         grad_inputs,

time: 1100 us -> 806 us (0.73)
  waiting for transfers between devices: 589 us -> 326 us
  blocking collectives: 57.1 us -> 0 us
  other arithmetic: 99.6 us -> 116 us
  local copies, waits for them, and re-layouts: 28.3 us -> 43.3 us
    reduce_scatter x5 -> x2, waiting for transfers between devices: 303 us -> 39.4 us  [the longest x1 39.4 us: shards(): lax.psum_scatter(pack_grad, 'grp', scatter_dimension=0, tiled=True)]
    all_gather x5 -> x4, waiting for transfers between devices: 13.3 us -> 62.4 us  [the longest x1 31.3 us: shards(): full_attn = lax.all_gather(pack_attn, 'grp', axis=0, tiled=True)]
    psum x1 -> x2, waiting for transfers between devices: 270 us -> 222 us  [the longest x1 148 us: shards(): shard_gu, shard_down = lax.psum((shard_gu, shard_down), 'rep')]
    psum x1 -> x0, blocking collectives: 23.2 us -> none  [shards(): lax.psum((shard_gain_attn, shard_query, shard_key, shard_value, shard_out...]
    all_gather x2 -> x0, blocking collectives: 19.7 us -> none  [the longest x1 11.5 us: shards(): lax.all_gather(w_key, 'grp', axis=0, tiled=True)]
    unnamed x2 -> x0, blocking collectives: 14.2 us -> none
    concatenate x0 -> x2, local copies, waits for them, and re-layouts: none -> 12.7 us  [the longest x1 9.22 us: shards(): jnp.concatenate([grad_wquery, grad_wkey, grad_wvalue, grad_wout, jnp.pad(...]
    unnamed x110 -> x107, local copies, waits for them, and re-layouts: 26.1 us -> 19.2 us
  transfers between devices with their start and end apart: 13 -> 9, of which waited for: 7 -> 5; matrix products, arithmetic and copies ran while one was open for 27% -> 46% of each run, Pallas kernels for 0% -> 0%
where the time goes in v1:
time: 806 us; the launch traced here: 802 us
  waiting for transfers between devices  326 us (40%)
  matrix products  303 us (38%)
  other arithmetic  116 us (14%)
  local copies, waits for them, and re-layouts  43.3 us (5%)
  between operations  14.9 us (2%)
    psum x1, waiting for transfers between devices, shards(): shard_gu, shard_down = lax.psum((shard_gu, shard_down), 'rep')  148 us
    psum x1, waiting for transfers between devices, shards(): shard_attn = lax.psum(shard_attn, 'rep').astype(jnp.float32)  73.8 us
    convert_element_type x2, other arithmetic, shards(): grad_scores = (probability * (grad_prob - inner)).astype(jnp.bfloat16)  56.1 us
    dot_general x7, matrix products, matmul(): return jnp.dot(left, right, preferred_element_type=jnp.float32)  52.7 us
    dot_general x2, matrix products, shards(): jnp.einsum('qkgd,tkd->kgqt', grad_block, values, preferred_element_type=j...  50.5 us
    dot_general x7, matrix products, right_product(): jnp.einsum('tf,ef->te', rows_grad, weight, preferred_element_type=jnp.flo...  41.3 us
    reduce_scatter x1, waiting for transfers between devices, shards(): lax.psum_scatter(pack_grad, 'grp', scatter_dimension=0, tiled=True)  39.4 us
    dot_general x7, matrix products, left_product(): jnp.einsum('te,tf->ef', rows_in, rows_grad, preferred_element_type=jnp.fl...  36.4 us
  transfers between devices with their start and end apart: 9, of which 5 were waited for; matrix products, arithmetic and copies ran while one was open for 46% of the time, Pallas kernels for 0%

profile of v1, /device:TPU:0, one launch (start us, length us, event | category | flops | bytes accessed | tf_op | source)
XLA Modules:
  0.0 802.5 jit_solution(5924584530543931098)
XLA Ops:
  11.8 3.5 concatenate.39
  19.8 31.1 %all-gather.11.cloned.1.call-done = bf16[2560,960]{0,1:T(8,128)(2,1)} async-done(((bf16[640,960]{0,1:T(8,128)(2,1)}), bf16[2560,960]{0,1:T(8,128)(2,1)}) %all-gather.11.cloned.1.call-update) | async-done | bytes 4915216 | tf_op jit(solution)/shard_map/all_gather | solution.py:122
  50.9 10.8 %fusion.81 = f32[1024,2560]{1,0:T(8,128)} fusion(bf16[1024,960]{0,1:T(8,128)(2,1)} %param.23, bf16[2560,960]{0,1:T(8,128)(2,1)} %all-gather.11.cloned.1.call-done), kind=kOutput, calls=%fused_computation.149 | convolution fusion | flops 5033164800 | bytes 17367040 | tf_op jit(solution)/shard_map/tf,ef->te/dot_general | solution.py:58
  61.7 31.3 %all-gather.5.cloned.1.call-done = bf16[960,2688]{1,0:T(8,128)(2,1)} async-done(((bf16[240,2688]{1,0:T(8,128)(2,1)}), bf16[960,2688]{1,0:T(8,128)(2,1)}) %all-gather.5.cloned.1.call-update) | async-done | bytes 5160976 | tf_op jit(solution)/shard_map/all_gather | solution.py:113
  94.6 2.8 fusion.62
  97.6 2.4 fusion.36
  100.8 13.0 %fusion.78 = (f32[5,3,512]{2,1,0:T(4,128)S(1)}, f32[5,3,512,1024]{2,3,1,0:T(8,128)}) fusion(bf16[512,5,3,64]{0,3,2,1:T(8,128)(2,1)S(1)} %bitcast.141, bf16[1024,5,32]{0,2,1:T(8,128)(2,1)S(1)} %get-tuple-element.93, bf16[1024,5,32]{0,2,1:T(8,128)(2,1)S(1)} %get-tuple-element.92, pred[512,1024]{0,1:T(8,128)(4,1)S(1)} %get-tuple-element.102), kind=kOutput, calls=%fused_computation.146 | convolution fusion | flops 1031528960 | bytes 33650688 | tf_op jit(solution)/shard_map/qkgd,tkd->kgqt/dot_general | solution.py:77
  113.8 12.8 %fusion.7 = f32[5,3,512]{2,1,0:T(4,128)S(1)} fusion(f32[5,3,512,1024]{2,3,1,0:T(8,128)} %get-tuple-element.106, f32[5,3,512]{2,1,0:T(4,128)S(1)} %get-tuple-element.105), kind=kLoop, calls=%fused_computation.19 | loop fusion | flops 15720960 | bytes 31518720 | tf_op jit(solution)/shard_map/reduce_sum | solution.py:147
  127.7 13.5 %fusion.53 = bf16[512,5,3,64]{0,3,2,1:T(8,128)(2,1)S(1)} fusion(bf16[1024,5,64,1]{0,2,3,1:T(8,128)(2,1)S(1)} %bitcast.148, f32[5,3,512,1024]{2,3,1,0:T(8,128)} %get-tuple-element.106, f32[5,3,512]{2,1,0:T(4,128)S(1)} %fusion.7, f32[5,3,512]{2,1,0:T(4,128)S(1)} %get-tuple-element.105), kind=kOutput, calls=%fused_computation.97 | convolution fusion | flops 1030717440 | bytes 33157120 | tf_op jit(solution)/shard_map/kgqt,tkd->qkgd/dot_general | solution.py:150
  141.3 12.8 %fusion.79 = (f32[5,3,512]{2,1,0:T(4,128)S(1)}, f32[5,3,512,1024]{2,3,1,0:T(8,128)}) fusion(bf16[512,5,3,64]{0,3,2,1:T(8,128)(2,1)S(1)} %bitcast.139, bf16[1024,5,32]{0,2,1:T(8,128)(2,1)S(1)} %get-tuple-element.93, bf16[1024,5,32]{0,2,1:T(8,128)(2,1)S(1)} %get-tuple-element.92, pred[512,1024]{0,1:T(8,128)(4,1)S(1)} %get-tuple-element.101), kind=kOutput, calls=%fused_computation.147 | convolution fusion | flops 1031528960 | bytes 33650688 | tf_op jit(solution)/shard_map/qkgd,tkd->kgqt/dot_general | solution.py:77
  154.0 12.9 %fusion.6 = f32[5,3,512]{2,1,0:T(4,128)S(1)} fusion(f32[5,3,512,1024]{2,3,1,0:T(8,128)} %get-tuple-element.108, f32[5,3,512]{2,1,0:T(4,128)S(1)} %get-tuple-element.107), kind=kLoop, calls=%fused_computation.18 | loop fusion | flops 15720960 | bytes 31518720 | tf_op jit(solution)/shard_map/reduce_sum | solution.py:147
  166.9 13.0 %fusion.52 = bf16[512,5,3,64]{0,3,2,1:T(8,128)(2,1)S(1)} fusion(bf16[1024,5,64,1]{0,2,3,1:T(8,128)(2,1)S(1)} %bitcast.149, f32[5,3,512,1024]{2,3,1,0:T(8,128)} %get-tuple-element.108, f32[5,3,512]{2,1,0:T(4,128)S(1)} %fusion.6, f32[5,3,512]{2,1,0:T(4,128)S(1)} %get-tuple-element.107), kind=kOutput, calls=%fused_computation.96 | convolution fusion | flops 1030717440 | bytes 33157120 | tf_op jit(solution)/shard_map/kgqt,tkd->qkgd/dot_general | solution.py:150
  180.2 5.4 multiply_reduce_fusion.2
  189.2 10.7 %fusion.80 = f32[1024,2560]{1,0:T(8,128)} fusion(bf16[1024,960]{0,1:T(8,128)(2,1)} %multiply_convert_fusion.3, bf16[960,2560]{1,0:T(8,128)(2,1)} %all-gather.9.cloned.1.call-done), kind=kOutput, calls=%fused_computation.148 | convolution fusion | flops 5033164800 | bytes 17367040 | tf_op jit(solution)/shard_map/dot_general | solution.py:50
  199.9 20.2 %multiply_convert_fusion.1 = (bf16[1024,2560]{1,0:T(8,128)(2,1)}, bf16[1024,2560]{1,0:T(8,128)(2,1)}, bf16[1024,2560]{1,0:T(8,128)(2,1)}) fusion(f32[1024,2560]{1,0:T(8,128)} %fusion.81, f32[1024,2560]{1,0:T(8,128)} %fusion.80, bf16[1024,960]{0,1:T(8,128)(2,1)} %multiply_convert_fusion.3, bf16[960,2560]{1,0:T(8,128)(2,1)} %all-gather.7.cloned.1.call-done), kind=kOutput, calls=%fused_computation.29 | convolution fusion | flops 5072486400 | bytes 43581440 | tf_op jit(solution)/shard_map/dot_general | solution.py:50
  220.1 8.1 %convolution_convert_fusion.1 = bf16[960,2560]{1,0:T(8,128)(2,1)S(1)} fusion(bf16[1024,960]{0,1:T(8,128)(2,1)S(1)} %copy-done.27, bf16[1024,2560]{1,0:T(8,128)(2,1)} %get-tuple-element.78), kind=kOutput, calls=%fused_computation.40 | convolution fusion | flops 5035622400 | bytes 12124160 | tf_op jit(solution)/shard_map/te,tf->ef/dot_general | solution.py:54
  228.2 5.5 convolution_convert_fusion.2
  233.8 8.9 %fusion.82 = f32[1024,960]{0,1:T(8,128)} fusion(bf16[1024,2560]{1,0:T(8,128)(2,1)} %get-tuple-element.77, bf16[960,2560]{1,0:T(8,128)(2,1)S(1)} %bitcast.171), kind=kOutput, calls=%fused_computation.150 | convolution fusion | flops 5033164800 | bytes 14090240 | tf_op jit(solution)/shard_map/tf,ef->te/dot_general | solution.py:58
  242.7 9.2 %multiply_reduce_fusion = (bf16[960]{0:T(1024)(128)(2,1)S(1)}, f32[1024]{0:T(1024)S(1)}, f32[1024,960]{0,1:T(8,128)}) fusion(f32[1024,960]{0,1:T(8,128)S(1)} %copy-done.2, f32[1024]{0:T(1024)S(1)} %add_rsqrt_fusion, f32[960]{0:T(1024)S(1)} %get-tuple-element.71, f32[1024,960]{0,1:T(8,128)} %fusion.82, bf16[1024,2560]{1,0:T(8,128)(2,1)S(1)} %copy-done.40, ...), kind=kOutput, calls=%fused_computation.54 | convolution fusion | flops 5040044032 | bytes 21968512 | tf_op jit(solution)/shard_map/tf,ef->te/dot_general | solution.py:58
  251.9 9.4 %convolution_convert_fusion = bf16[2560,960]{0,1:T(8,128)(2,1)} fusion(bf16[1024,960]{0,1:T(8,128)(2,1)S(1)} %copy-done.23, bf16[1024,2560]{1,0:T(8,128)(2,1)} %get-tuple-element.79), kind=kOutput, calls=%fused_computation.39 | convolution fusion | flops 5035622400 | bytes 12124160 | tf_op jit(solution)/shard_map/te,tf->ef/dot_general | solution.py:54
  261.3 4.5 pad_maximum_fusion
  265.8 6.9 multiply_add_fusion
  272.7 7.9 copy.100
  281.4 5.0 convolution_convert_fusion.3
  286.6 16.1 %fusion.40 = f32[5,64,1024]{2,1,0:T(8,128)} fusion(bf16[512,5,3,64]{0,3,2,1:T(8,128)(2,1)S(1)} %bitcast.143, f32[5,3,512,1024]{2,3,1,0:T(8,128)} %get-tuple-element.108, f32[5,3,512]{2,1,0:T(4,128)S(1)} %log_add_fusion.1), kind=kOutput, calls=%fused_computation.87 | convolution fusion | flops 1022361600 | bytes 33781760 | tf_op jit(solution)/shard_map/kgqt,qkgd->tkd/dot_general | solution.py:212
  302.7 13.9 %fusion.49 = bf16[5,64,1024]{2,1,0:T(8,128)(2,1)} fusion(f32[5,64,1024]{2,1,0:T(8,128)} %fusion.40, bf16[512,5,3,64]{0,3,2,1:T(8,128)(2,1)S(1)} %bitcast.145, f32[5,3,512,1024]{2,3,1,0:T(8,128)} %get-tuple-element.106, f32[5,3,512]{2,1,0:T(4,128)S(1)} %log_add_fusion), kind=kOutput, calls=%fused_computation.92 | convolution fusion | flops 1023016960 | bytes 34437120 | tf_op jit(solution)/shard_map/kgqt,qkgd->tkd/dot_general | solution.py:212
  316.7 2.9 convolution_convert_fusion.6
  319.5 2.2 copy.83
  321.9 26.7 %fusion = (f32[5,3,512]{2,1,0:T(4,128)S(1)}, f32[5,1024,512,3]{2,1,3,0:T(8,128)}) fusion(f32[5,3,512,1024]{2,3,1,0:T(8,128)} %get-tuple-element.106, f32[5,3,512]{2,1,0:T(4,128)S(1)} %log_add_fusion, bf16[1024,5,64,1]{0,2,3,1:T(8,128)(2,1)} %bitcast.150, bf16[512,5,3,64]{0,3,2,1:T(8,128)(2,1)} %bitcast.146), kind=kOutput, calls=%fused_computation.2 | convolution fusion | flops 1030218240 | bytes 64614400 | tf_op jit(solution)/shard_map/qkgd,tkd->kgqt/dot_general | solution.py:196
  348.6 28.7 %fusion.2 = bf16[5,3,512,1024]{2,3,1,0:T(8,128)(2,1)} fusion(f32[5,1024,512,3]{2,1,3,0:T(8,128)} %get-tuple-element.113, f32[5,3,512,1024]{2,3,1,0:T(8,128)} %get-tuple-element.106, f32[5,3,512]{2,1,0:T(4,128)S(1)} %get-tuple-element.112, f32[5,3,512]{2,1,0:T(4,128)S(1)} %log_add_fusion), kind=kLoop, calls=%fused_computation.4 | loop fusion | flops 31457280 | bytes 78704640 | tf_op jit(solution)/shard_map/convert_element_type | solution.py:200
  377.3 11.5 %convolution_bitcast_fusion = f32[5,64,1024]{2,1,0:T(8,128)} fusion(bf16[512,5,3,64]{0,3,2,1:T(8,128)(2,1)S(1)} %bitcast.142, bf16[5,3,512,1024]{2,3,1,0:T(8,128)(2,1)} %fusion.2), kind=kOutput, calls=%fused_computation.89 | convolution fusion | flops 1006632960 | bytes 18022400 | tf_op jit(solution)/shard_map/kgqt,qkgd->tkd/dot_general | solution.py:207
  388.8 23.8 %fusion.3 = (f32[5,3,512]{2,1,0:T(4,128)S(1)}, f32[5,1024,512,3]{2,1,3,0:T(8,128)}) fusion(f32[5,3,512,1024]{2,3,1,0:T(8,128)} %get-tuple-element.108, f32[5,3,512]{2,1,0:T(4,128)S(1)} %log_add_fusion.1, bf16[1024,5,64,1]{0,2,3,1:T(8,128)(2,1)S(1)} %bitcast.151, bf16[512,5,3,64]{0,3,2,1:T(8,128)(2,1)S(1)} %bitcast.144), kind=kOutput, calls=%fused_computation.7 | convolution fusion | flops 1030218240 | bytes 64614400 | tf_op jit(solution)/shard_map/qkgd,tkd->kgqt/dot_general | solution.py:196
  412.7 27.4 %fusion.5 = bf16[5,3,512,1024]{2,3,1,0:T(8,128)(2,1)} fusion(f32[5,1024,512,3]{2,1,3,0:T(8,128)} %get-tuple-element.115, f32[5,3,512,1024]{2,3,1,0:T(8,128)} %get-tuple-element.108, f32[5,3,512]{2,1,0:T(4,128)S(1)} %get-tuple-element.114, f32[5,3,512]{2,1,0:T(4,128)S(1)} %log_add_fusion.1), kind=kLoop, calls=%fused_computation.9 | loop fusion | flops 31457280 | bytes 78704640 | tf_op jit(solution)/shard_map/convert_element_type | solution.py:200
  440.1 11.4 %fusion.56 = f32[1024,5,64]{0,2,1:T(8,128)} fusion(f32[5,64,1024]{2,1,0:T(8,128)S(1)} %copy-done.14, bf16[512,5,3,64]{0,3,2,1:T(8,128)(2,1)S(1)} %bitcast.140, bf16[5,3,512,1024]{2,3,1,0:T(8,128)(2,1)} %fusion.5), kind=kOutput, calls=%fused_computation.100 | convolution fusion | flops 1007288320 | bytes 19333120 | tf_op jit(solution)/shard_map/kgqt,qkgd->tkd/dot_general | solution.py:207
  454.9 2.2 copy.82
  457.1 8.3 %multiply_bitcast_fusion = f32[512,5,3,64]{0,3,2,1:T(8,128)S(1)} fusion(bf16[5,3,512,1024]{2,3,1,0:T(8,128)(2,1)} %fusion.2, bf16[1024,5,32]{0,2,1:T(8,128)(2,1)S(1)} %copy-done.13, bf16[1024,5,32]{0,2,1:T(8,128)(2,1)S(1)} %copy-done.11), kind=kOutput, calls=%fused_computation.71 | convolution fusion | flops 1008435200 | bytes 18350080 | tf_op jit(solution)/shard_map/kgqt,tkd->qkgd/dot_general | solution.py:202
  465.4 8.3 %multiply_bitcast_fusion.1 = f32[512,5,3,64]{0,3,2,1:T(8,128)S(1)} fusion(bf16[5,3,512,1024]{2,3,1,0:T(8,128)(2,1)} %fusion.5, bf16[1024,5,32]{0,2,1:T(8,128)(2,1)S(1)} %copy-done.13, bf16[1024,5,32]{0,2,1:T(8,128)(2,1)S(1)} %copy-done.11), kind=kOutput, calls=%fused_computation.72 | convolution fusion | flops 1008435200 | bytes 18350080 | tf_op jit(solution)/shard_map/kgqt,tkd->qkgd/dot_general | solution.py:202
  480.0 3.9 fusion.29
  484.9 5.2 convolution_convert_fusion.5
  490.1 3.5 convolution_convert_fusion.4
  493.6 9.2 %concatenate.49 = bf16[960,2688]{1,0:T(8,128)(2,1)} concatenate(bf16[960,960]{1,0:T(8,128)(2,1)} %convolution_convert_fusion.5, bf16[960,320]{1,0:T(8,128)(2,1)S(1)} %copy-done.18, bf16[960,320]{1,0:T(8,128)(2,1)S(1)} %copy-done.17, bf16[960,960]{1,0:T(8,128)(2,1)} %convolution_convert_fusion.4, bf16[960,128]{1,0:T(8,128)(2,1)} %pad.10), dimensions={1} | concatenate | bytes 10321920 | tf_op jit(solution)/shard_map/concatenate | solution.py:231
  502.9 2.4 copy.101
  505.4 10.3 %add_convert_fusion = bf16[1024,960]{0,1:T(8,128)(2,1)} fusion(f32[1024,960]{0,1:T(8,128)} %copy-done.1, bf16[1024,2560]{1,0:T(8,128)(2,1)} %get-tuple-element.79, bf16[2560,960]{0,1:T(8,128)(2,1)} %all-gather.11.cloned.1.call-done), kind=kOutput, calls=%fused_computation.58 | convolution fusion | flops 5035130880 | bytes 16056320 | tf_op jit(solution)/shard_map/dot_general | solution.py:50
  515.7 39.4 %reduce-scatter.6.cloned.1.call-done = bf16[240,2688]{1,0:T(8,128)(2,1)} async-done(((bf16[960,2688]{1,0:T(8,128)(2,1)}), bf16[240,2688]{1,0:T(8,128)(2,1)}) %reduce-scatter.6.cloned.1.call-update) | async-done | bytes 1290256 | tf_op jit(solution)/shard_map/reduce_scatter | solution.py:241
  555.1 148.1 %all-reduce.8.cloned.1.call-done = (bf16[240,5120]{1,0:T(8,128)(2,1)}, bf16[640,960]{0,1:T(8,128)(2,1)}) async-done(((bf16[240,5120]{1,0:T(8,128)(2,1)}, bf16[640,960]{0,1:T(8,128)(2,1)}), (bf16[240,5120]{1,0:T(8,128)(2,1)}, bf16[640,960]{0,1:T(8,128)(2,1)})) %all-reduce.8.cloned.1.call-update) | async-done | bytes 3686416 | tf_op jit(solution)/shard_map/psum | solution.py:181
  703.2 6.4 fusion.25
  712.2 2.9 slice_convert_fusion
  715.1 73.8 %all-reduce.6.cloned.1.call-done = bf16[240,2688]{1,0:T(8,128)(2,1)} async-done(((bf16[240,2688]{1,0:T(8,128)(2,1)}), bf16[240,2688]{1,0:T(8,128)(2,1)}) %all-reduce.6.cloned.1.call-update) | async-done | bytes 1290256 | tf_op jit(solution)/shard_map/psum | solution.py:243
  (180 shorter events, 37.7 us)
Async XLA Ops:
  7.2 43.7 %all-gather.11.cloned.1.call-start = ((), (), s32[]{:S(2)}) async-start(), calls=%async_computation.6 | async-start | bytes 6144000 | tf_op jit(solution)/shard_map/all_gather | solution.py:122
  7.9 8.8 %copy-start.34 = (s32[1,1024]{1,0:T(1,128)S(1)}, s32[1,1024]{1,0:T(1,128)}, u32[]{:S(2)}) copy-start(s32[1,1024]{1,0:T(1,128)} %param.13) | copy-start | bytes 12292
  7.9 9.5 %copy-start = (bf16[1024,960]{0,1:T(8,128)(2,1)S(1)}, bf16[1024,960]{0,1:T(8,128)(2,1)}, u32[]{:S(2)}) copy-start(bf16[1024,960]{0,1:T(8,128)(2,1)} %param.12) | copy-start | bytes 5898244
  7.9 85.1 %all-gather.5.cloned.1.call-start = ((), (), s32[]{:S(2)}) async-start(), calls=%async_computation.3 | async-start | bytes 6451200 | tf_op jit(solution)/shard_map/all_gather | solution.py:113
  15.3 173.9 %all-gather.9.cloned.1.call-start = ((), (), s32[]{:S(2)}) async-start(), calls=%async_computation.5 | async-start | bytes 6144000 | tf_op jit(solution)/shard_map/all_gather | solution.py:121
  16.0 183.8 %all-gather.7.cloned.1.call-start = ((), (), s32[]{:S(2)}) async-start(), calls=%async_computation.4 | async-start | bytes 6144000 | tf_op jit(solution)/shard_map/all_gather | solution.py:120
  16.6 486.3 %reduce-scatter.10.cloned.1.call-start = ((), (), s32[]{:S(2)}) async-start(), calls=%async_computation.10 | async-start | bytes 6553600
  17.9 108.8 %copy-start.37 = (f32[1024]{0:T(1024)}, f32[1024]{0:T(1024)S(1)}, u32[]{:S(2)}) copy-start(f32[1024]{0:T(1024)S(1)} %add_rsqrt_fusion.1) | copy-start | bytes 12292
  19.1 80.9 %copy-start.15 = (f32[1024,32]{0,1:T(8,128)}, f32[1024,32]{0,1:T(8,128)S(1)}, u32[]{:S(2)}) copy-start(f32[1024,32]{0,1:T(8,128)S(1)} %get-tuple-element.100) | copy-start | bytes 393220
  93.0 4.5 slice-start
  94.5 32.2 %copy-start.35 = (f32[960]{0:T(1024)}, f32[960]{0:T(1024)S(1)}, u32[]{:S(2)}) copy-start(f32[960]{0:T(1024)S(1)} %get-tuple-element.72) | copy-start | bytes 11524
  97.6 43.7 %copy-start.10 = (bf16[1024,5,32]{0,2,1:T(8,128)(2,1)}, bf16[1024,5,32]{0,2,1:T(8,128)(2,1)S(1)}, u32[]{:S(2)}) copy-start(bf16[1024,5,32]{0,2,1:T(8,128)(2,1)S(1)} %get-tuple-element.92) | copy-start | bytes 983044
  97.6 43.7 %copy-start.12 = (bf16[1024,5,32]{0,2,1:T(8,128)(2,1)}, bf16[1024,5,32]{0,2,1:T(8,128)(2,1)S(1)}, u32[]{:S(2)}) copy-start(bf16[1024,5,32]{0,2,1:T(8,128)(2,1)S(1)} %get-tuple-element.93) | copy-start | bytes 983044
  100.8 13.0 %copy-start.7 = (bf16[512,15,64]{0,2,1:T(8,128)(2,1)}, bf16[512,15,64]{0,2,1:T(8,128)(2,1)S(1)}, u32[]{:S(2)}) copy-start(bf16[512,15,64]{0,2,1:T(8,128)(2,1)S(1)} %get-tuple-element.89) | copy-start | bytes 2949124
  100.8 40.4 %copy-start.5 = (bf16[512,15,64]{0,2,1:T(8,128)(2,1)}, bf16[512,15,64]{0,2,1:T(8,128)(2,1)S(1)}, u32[]{:S(2)}) copy-start(bf16[512,15,64]{0,2,1:T(8,128)(2,1)S(1)} %get-tuple-element.88) | copy-start | bytes 2949124
  113.8 13.9 %copy-start.30 = (f32[5,3,512]{2,1,0:T(4,128)}, f32[5,3,512]{2,1,0:T(4,128)S(1)}, u32[]{:S(2)}) copy-start(f32[5,3,512]{2,1,0:T(4,128)S(1)} %get-tuple-element.105) | copy-start | bytes 92164
  127.7 39.2 %copy-start.19 = (bf16[1024,320]{0,1:T(8,128)(2,1)}, bf16[1024,320]{0,1:T(8,128)(2,1)S(1)}, u32[]{:S(2)}) copy-start(bf16[1024,320]{0,1:T(8,128)(2,1)S(1)} %convolution_convert_fusion.8) | copy-start | bytes 1966084
  180.2 5.4 copy-start.24
  199.9 20.2 %copy-start.27 = (bf16[1024,960]{0,1:T(8,128)(2,1)S(1)}, bf16[1024,960]{0,1:T(8,128)(2,1)}, u32[]{:S(2)}) copy-start(bf16[1024,960]{0,1:T(8,128)(2,1)} %multiply_convert_fusion.3) | copy-start | bytes 5898244
  220.1 8.1 %copy-start.41 = (bf16[1024,2560]{1,0:T(8,128)(2,1)S(1)}, bf16[1024,2560]{1,0:T(8,128)(2,1)}, u32[]{:S(2)}) copy-start(bf16[1024,2560]{1,0:T(8,128)(2,1)} %get-tuple-element.77) | copy-start | bytes 15728644
  220.1 13.6 %slice-start.6 = ((s8[4915200]{0:T(1024)(128)(4,1)}), s8[4194304]{0:T(1024)(128)(4,1)S(1)}, s32[]{:S(2)}) async-start(s8[4915200]{0:T(1024)(128)(4,1)} %bitcast.170), calls=%async_computation.18 | async-start | bytes 8388608
  220.1 22.6 %slice-start.4 = ((s8[4915200]{0:T(1024)(128)(4,1)}), s8[4194304]{0:T(1024)(128)(4,1)S(1)}, s32[]{:S(2)}) async-start(s8[4915200]{0:T(1024)(128)(4,1)} %bitcast.168), calls=%async_computation.16 | async-start | bytes 8388608
  228.2 5.5 slice-start.7
  228.2 14.5 %slice-start.5 = ((s8[4915200]{0:T(1024)(128)(4,1)}), s8[720896]{0:T(1024)(128)(4,1)S(1)}, s32[]{:S(2)}) async-start(s8[4915200]{0:T(1024)(128)(4,1)} %bitcast.168), calls=%async_computation.17 | async-start | bytes 1441792
  233.7 8.9 %copy-start.2 = (f32[1024,960]{0,1:T(8,128)S(1)}, f32[1024,960]{0,1:T(8,128)}, u32[]{:S(2)}) copy-start(f32[1024,960]{0,1:T(8,128)} %copy-done.1) | copy-start | bytes 11796484
  233.8 8.9 %copy-start.40 = (bf16[1024,2560]{1,0:T(8,128)(2,1)S(1)}, bf16[1024,2560]{1,0:T(8,128)(2,1)}, u32[]{:S(2)}) copy-start(bf16[1024,2560]{1,0:T(8,128)(2,1)} %get-tuple-element.78) | copy-start | bytes 15728644
  242.7 9.2 %copy-start.23 = (bf16[1024,960]{0,1:T(8,128)(2,1)S(1)}, bf16[1024,960]{0,1:T(8,128)(2,1)}, u32[]{:S(2)}) copy-start(bf16[1024,960]{0,1:T(8,128)(2,1)} %param.23) | copy-start | bytes 5898244
  280.6 224.8 %reduce-scatter.8.cloned.1.call-start = ((), (), s32[]{:S(2)}) async-start(), calls=%async_computation.8 | async-start | bytes 12288000 | tf_op jit(solution)/shard_map/reduce_scatter | solution.py:179
  286.6 16.1 %copy-start.9 = (bf16[512,960]{0,1:T(8,128)(2,1)}, bf16[512,960]{0,1:T(8,128)(2,1)S(1)}, u32[]{:S(2)}) copy-start(bf16[512,960]{0,1:T(8,128)(2,1)S(1)} %get-tuple-element.87) | copy-start | bytes 2949124
  302.7 14.0 %copy-start.36 = (f32[960]{0:T(1024)S(1)}, f32[960]{0:T(1024)}, u32[]{:S(2)}) copy-start(f32[960]{0:T(1024)} %copy-done.35) | copy-start | bytes 11524
  302.7 14.0 %copy-start.38 = (f32[1024]{0:T(1024)S(1)}, f32[1024]{0:T(1024)}, u32[]{:S(2)}) copy-start(f32[1024]{0:T(1024)} %copy-done.37) | copy-start | bytes 12292
  321.8 233.3 %reduce-scatter.6.cloned.1.call-start = ((), (), s32[]{:S(2)}) async-start(), calls=%async_computation.7 | async-start | bytes 6451200 | tf_op jit(solution)/shard_map/reduce_scatter | solution.py:241
  348.5 28.8 %copy-start.8 = (bf16[512,15,64]{0,2,1:T(8,128)(2,1)S(1)}, bf16[512,15,64]{0,2,1:T(8,128)(2,1)}, u32[]{:S(2)}) copy-start(bf16[512,15,64]{0,2,1:T(8,128)(2,1)} %copy-done.7) | copy-start | bytes 2949124
  377.3 11.5 %copy-start.20 = (bf16[1024,320]{0,1:T(8,128)(2,1)S(1)}, bf16[1024,320]{0,1:T(8,128)(2,1)}, u32[]{:S(2)}) copy-start(bf16[1024,320]{0,1:T(8,128)(2,1)} %copy-done.19) | copy-start | bytes 1966084
  412.6 27.4 %copy-start.6 = (bf16[512,15,64]{0,2,1:T(8,128)(2,1)S(1)}, bf16[512,15,64]{0,2,1:T(8,128)(2,1)}, u32[]{:S(2)}) copy-start(bf16[512,15,64]{0,2,1:T(8,128)(2,1)} %copy-done.5) | copy-start | bytes 2949124
  412.6 27.4 %copy-start.14 = (f32[5,64,1024]{2,1,0:T(8,128)S(1)}, f32[5,64,1024]{2,1,0:T(8,128)}, u32[]{:S(2)}) copy-start(f32[5,64,1024]{2,1,0:T(8,128)} %convolution_bitcast_fusion) | copy-start | bytes 3932164
  440.1 11.4 %copy-start.16 = (f32[1024,32]{0,1:T(8,128)S(1)}, f32[1024,32]{0,1:T(8,128)}, u32[]{:S(2)}) copy-start(f32[1024,32]{0,1:T(8,128)} %copy-done.15) | copy-start | bytes 393220
  440.1 11.4 %copy-start.29 = (f32[1024,32]{0,1:T(8,128)S(1)}, f32[1024,32]{0,1:T(8,128)}, u32[]{:S(2)}) copy-start(f32[1024,32]{0,1:T(8,128)} %get-tuple-element.98) | copy-start | bytes 393220
  453.1 4.1 copy-start.11
  453.1 4.1 copy-start.13
  480.0 3.9 copy-start.39
  484.9 5.2 copy-start.3
  484.9 5.2 copy-start.25
  490.1 3.5 copy-start.18
  502.9 200.3 %all-reduce.8.cloned.1.call-start = ((), (), s32[]{:S(2)}) async-start(), calls=%async_computation.11 | async-start | bytes 7372800 | tf_op jit(solution)/shard_map/psum | solution.py:181
  505.4 283.5 %all-reduce.6.cloned.1.call-start = ((), (), s32[]{:S(2)}) async-start(), calls=%async_computation.9 | async-start | bytes 2580480 | tf_op jit(solution)/shard_map/psum | solution.py:243
  703.2 6.4 copy-start.28
  788.9 5.3 copy-start.4
  (11 other events, 21.8 us)
Sparse Core Ops, SparseCore 0:
  9.6 41.2 all-gather.10
  53.0 39.9 all-gather.4
  94.6 38.5 all-gather.8
  134.6 38.5 all-gather.6
  280.7 52.5 reduce-scatter.9
  336.0 80.8 reduce-scatter.7
  503.0 52.0 reduce-scatter.5
  559.4 143.7 all-reduce.7
  706.8 82.0 all-reduce.5

commit v2 on v1

--- a/solution.py
+++ b/solution.py
@@ -1,11 +1,15 @@
 import jax
 import jax.numpy as jnp
 from jax import lax
+from jax.experimental import pallas as pl
+from jax.experimental.pallas import tpu as pltpu
 from jax.sharding import PartitionSpec as P
 
 QH = 15
 KVH = 5
 HD = 64
+BLOCK = 256
+DOC_MAX = 512
 
 
 EPS = 1e-05
@@ -67,19 +71,119 @@
     return (grad_gain, grad_values)
 
 
-def block_scores(query_block, keys, segment_row, offset, scale):
-    block = query_block.shape[0]
-    length = keys.shape[0]
-    query_places = offset + jnp.arange(block, dtype=jnp.int32)
-    key_places = jnp.arange(length, dtype=jnp.int32)
-    query_segments = segment_row[offset : offset + block]
-    scores = (
-        jnp.einsum("qkgd,tkd->kgqt", query_block, keys, preferred_element_type=jnp.float32) * scale
-    )
-    allowed = (query_segments[:, None] == segment_row[None, :]) & (
-        key_places[None, :] <= query_places[:, None]
-    )
-    return jnp.where(allowed, scores, -1e30)
+def dot_kernel(left, right, dims):
+    return lax.dot_general(left, right, (((dims[0],), (dims[1],)), ((), ())), preferred_element_type=jnp.float32)
+
+
+def allowed_block(seg_col, seg_row, low, start, stop):
+    query_places = start + lax.broadcasted_iota(jnp.int32, (stop - start, stop - low), 0)
+    key_places = low + lax.broadcasted_iota(jnp.int32, (stop - start, stop - low), 1)
+    same = seg_col[start:stop, :] == seg_row[:, low:stop]
+    return same & (key_places <= query_places)
+
+
+def windows(length):
+    block = min(BLOCK, length)
+    for start in range(0, length, block):
+        yield max(0, start - DOC_MAX), start, start + block
+
+
+def attend_kernel(q_ref, k_ref, v_ref, col_ref, row_ref, o_ref, lse_ref):
+    scale = HD ** (-0.5)
+    for low, start, stop in windows(q_ref.shape[2]):
+        allowed = allowed_block(col_ref, row_ref, low, start, stop)
+        keys = k_ref[0, low:stop, :]
+        values = v_ref[0, low:stop, :]
+        for head in range(q_ref.shape[1]):
+            scores = dot_kernel(q_ref[0, head, start:stop, :], keys, (1, 1)) * scale
+            scores = jnp.where(allowed, scores, -1e30)
+            peak = jnp.max(scores, axis=-1, keepdims=True)
+            exponent = jnp.exp(scores - peak)
+            totals = jnp.sum(exponent, axis=-1, keepdims=True)
+            probability = (exponent * (1.0 / totals)).astype(jnp.bfloat16)
+            o_ref[0, head, start:stop, :] = dot_kernel(probability, values, (1, 0)).astype(
+                jnp.bfloat16
+            )
+            lse_ref[0, head, start:stop, :] = peak + jnp.log(totals)
+
+
+def attend_back_kernel(
+    q_ref, k_ref, v_ref, do_ref, lse_ref, col_ref, row_ref, dq_ref, dk_ref, dv_ref
+):
+    scale = HD ** (-0.5)
+    dk_ref[...] = jnp.zeros_like(dk_ref)
+    dv_ref[...] = jnp.zeros_like(dv_ref)
+    for low, start, stop in windows(q_ref.shape[2]):
+        allowed = allowed_block(col_ref, row_ref, low, start, stop)
+        keys = k_ref[0, low:stop, :]
+        values = v_ref[0, low:stop, :]
+        grad_keys = jnp.zeros((stop - low, HD), jnp.float32)
+        grad_values = jnp.zeros((stop - low, HD), jnp.float32)
+        for head in range(q_ref.shape[1]):
+            queries = q_ref[0, head, start:stop, :]
+            grads = do_ref[0, head, start:stop, :]
+            scores = dot_kernel(queries, keys, (1, 1)) * scale
+            probability = jnp.exp(
+                jnp.where(allowed, scores, -1e30) - lse_ref[0, head, start:stop, :]
+            )
+            grad_prob = dot_kernel(grads, values, (1, 1))
+            inner = jnp.sum(probability * grad_prob, axis=-1, keepdims=True)
+            grad_scores = (probability * (grad_prob - inner)).astype(jnp.bfloat16)
+            dq_ref[0, head, start:stop, :] = dot_kernel(grad_scores, keys, (1, 0)) * scale
+            grad_keys += dot_kernel(grad_scores, queries, (0, 0))
+            grad_values += dot_kernel(probability.astype(jnp.bfloat16), grads, (0, 0))
+        dk_ref[0, low:stop, :] += grad_keys * scale
+        dv_ref[0, low:stop, :] += grad_values
+
+
+def head_specs(length, groups):
+    heads = pl.BlockSpec((1, groups, length, HD), lambda i: (i, 0, 0, 0))
+    narrow = pl.BlockSpec((1, groups, length, 1), lambda i: (i, 0, 0, 0))
+    shared = pl.BlockSpec((1, length, HD), lambda i: (i, 0, 0))
+    column = pl.BlockSpec((length, 1), lambda i: (0, 0))
+    row = pl.BlockSpec((1, length), lambda i: (0, 0))
+    return heads, narrow, shared, column, row
+
+
+def attend(q, k, v, segments):
+    kvh, groups, length, _ = q.shape
+    heads, narrow, shared, column, row = head_specs(length, groups)
+    return pl.pallas_call(
+        attend_kernel,
+        grid=(kvh,),
+        out_shape=(
+            jax.ShapeDtypeStruct(q.shape, jnp.bfloat16),
+            jax.ShapeDtypeStruct((kvh, groups, length, 1), jnp.float32),
+        ),
+        in_specs=[heads, shared, shared, column, row],
+        out_specs=(heads, narrow),
+        compiler_params=pltpu.CompilerParams(vmem_limit_bytes=40 * 1024 * 1024),
+        cost_estimate=pl.CostEstimate(
+            flops=20_000_000_000, bytes_accessed=20_000_000, transcendentals=8_000_000
+        ),
+        name="attend",
+    )(q, k, v, segments.reshape(length, 1), segments)
+
+
+def attend_back(q, k, v, grads, lse, segments):
+    kvh, groups, length, _ = q.shape
+    heads, narrow, shared, column, row = head_specs(length, groups)
+    return pl.pallas_call(
+        attend_back_kernel,
+        grid=(kvh,),
+        out_shape=(
+            jax.ShapeDtypeStruct(q.shape, jnp.float32),
+            jax.ShapeDtypeStruct(k.shape, jnp.float32),
+            jax.ShapeDtypeStruct(k.shape, jnp.float32),
+        ),
+        in_specs=[heads, shared, shared, heads, narrow, column, row],
+        out_specs=(heads, shared, shared),
+        compiler_params=pltpu.CompilerParams(vmem_limit_bytes=48 * 1024 * 1024),
+        cost_estimate=pl.CostEstimate(
+            flops=50_000_000_000, bytes_accessed=30_000_000, transcendentals=8_000_000
+        ),
+        name="attend_back",
+    )(q, k, v, grads, lse, segments.reshape(length, 1), segments)
 
 
 def shards(
@@ -122,8 +226,6 @@
     down_full = lax.all_gather(w_down, "grp", axis=0, tiled=True)
     length = tokens.shape[0]
     groups = QH // KVH
-    scale = HD ** (-0.5)
-    block = min(512, length)
     segment_row = segments[0]
     cosine, sine = rope_tables(positions_of(segment_row), HD)
     inputs = tokens.astype(jnp.float32)
@@ -136,21 +238,11 @@
         jnp.bfloat16
     )
     values = matmul(normed_attn, value_full).astype(jnp.bfloat16).reshape(length, KVH, HD)
-    query_blocks = queries.reshape(length, KVH, groups, HD)
-    outputs = []
-    log_totals = []
-    for offset in range(0, length, block):
-        query_block = query_blocks[offset : offset + block]
-        scores = block_scores(query_block, keys, segment_row, offset, scale)
-        row_peak = jnp.max(scores, axis=-1, keepdims=True)
-        exponent = jnp.exp(scores - row_peak)
-        totals = jnp.sum(exponent, axis=-1, keepdims=True)
-        probability = (exponent / totals).astype(jnp.bfloat16)
-        outputs.append(
-            jnp.einsum("kgqt,tkd->qkgd", probability, values, preferred_element_type=jnp.float32)
-        )
-        log_totals.append(row_peak + jnp.log(totals))
-    attended = jnp.concatenate(outputs, axis=0).reshape(length, QH * HD).astype(jnp.bfloat16)
+    query_heads = queries.reshape(length, KVH, groups, HD).transpose(1, 2, 0, 3)
+    key_heads = keys.transpose(1, 0, 2)
+    value_heads = values.transpose(1, 0, 2)
+    attended, log_totals = attend(query_heads, key_heads, value_heads, segments)
+    attended = attended.transpose(2, 0, 1, 3).reshape(length, QH * HD)
     residual = inputs + matmul(attended, out_full)
     scale_mlp = rms_scale(residual)
     normed_mlp = (residual * scale_mlp * gain_mlp.astype(jnp.float32)).astype(jnp.bfloat16)
@@ -182,37 +274,17 @@
     grad_attn = grad_residual.astype(jnp.bfloat16)
     grad_wout = left_product(attended, grad_attn)
     grad_attended = (
-        right_product(grad_attn, out_full).astype(jnp.bfloat16).reshape(length, KVH, groups, HD)
-    )
-    grad_keys = jnp.zeros((length, KVH, HD), jnp.float32)
-    grad_values = jnp.zeros((length, KVH, HD), jnp.float32)
-    grad_query_blocks = []
-    for index, offset in enumerate(range(0, length, block)):
-        query_block = query_blocks[offset : offset + block]
-        grad_block = grad_attended[offset : offset + block]
-        scores = block_scores(query_block, keys, segment_row, offset, scale)
-        probability = jnp.exp(scores - log_totals[index])
-        prob_low = probability.astype(jnp.bfloat16)
-        grad_prob = jnp.einsum(
-            "qkgd,tkd->kgqt", grad_block, values, preferred_element_type=jnp.float32
-        )
-        inner = jnp.sum(probability * grad_prob, axis=-1, keepdims=True)
-        grad_scores = (probability * (grad_prob - inner)).astype(jnp.bfloat16)
-        grad_query_blocks.append(
-            jnp.einsum("kgqt,tkd->qkgd", grad_scores, keys, preferred_element_type=jnp.float32)
-            * scale
-        )
-        grad_keys = (
-            grad_keys
-            + jnp.einsum(
-                "kgqt,qkgd->tkd", grad_scores, query_block, preferred_element_type=jnp.float32
-            )
-            * scale
-        )
-        grad_values = grad_values + jnp.einsum(
-            "kgqt,qkgd->tkd", prob_low, grad_block, preferred_element_type=jnp.float32
-        )
-    grad_query_rot = jnp.concatenate(grad_query_blocks, axis=0).reshape(length, QH, HD)
+        right_product(grad_attn, out_full)
+        .astype(jnp.bfloat16)
+        .reshape(length, KVH, groups, HD)
+        .transpose(1, 2, 0, 3)
+    )
+    grad_query_rot, grad_keys, grad_values = attend_back(
+        query_heads, key_heads, value_heads, grad_attended, log_totals, segments
+    )
+    grad_query_rot = grad_query_rot.transpose(2, 0, 1, 3).reshape(length, QH, HD)
+    grad_keys = grad_keys.transpose(1, 0, 2)
+    grad_values = grad_values.transpose(1, 0, 2)
     grad_queries = (
         rotate(grad_query_rot, cosine, -sine).reshape(length, QH * HD).astype(jnp.bfloat16)
     )

time: 806 us -> 711 us (0.88)
  matrix products: 303 us -> 137 us
  other arithmetic: 116 us -> 39.6 us
  Pallas kernels: 0 us -> 72.5 us
  local copies, waits for them, and re-layouts: 43.3 us -> 104 us
    dot_general x12 -> x0, matrix products: 172 us -> none  [the longest x2 50.5 us: shards(): jnp.einsum('qkgd,tkd->kgqt', grad_block, values, preferred_element_type=j...]
    pallas_call x0 -> x2, Pallas kernels: none -> 72.5 us  [the longest x1 43.3 us: attend_back(): pl.pallas_call(attend_back_kernel, grid=(kvh,), out_shape=(jax.ShapeDtype...]
    convert_element_type x2 -> x1, other arithmetic: 56.1 us -> 1.95 us  [shards(): grad_values_low = grad_values.reshape(length, KVH * HD).astype(jnp.bfloat16)]
    reduce_sum x2 -> x0, other arithmetic: 25.7 us -> none  [shards(): totals = jnp.sum(exponent, axis=-1, keepdims=True)]
    unnamed x107 -> x87, local copies, waits for them, and re-layouts: 19.2 us -> 38.9 us
    slice x3, local copies, waits for them, and re-layouts: 0.21 us -> 17.2 us  [the longest x2 17.1 us: rotate(): second_half = values[..., halfway:]]
  transfers between devices with their start and end apart: 9 -> 9, of which waited for: 5 -> 6; matrix products, arithmetic and copies ran while one was open for 46% -> 27% of each run, Pallas kernels for 0% -> 10%
where the time goes in v2:
time: 711 us; the launch traced here: 701 us
  waiting for transfers between devices  333 us (47%)
  matrix products  137 us (19%)
  local copies, waits for them, and re-layouts  104 us (15%)
  Pallas kernels  72.5 us (10%)
  other arithmetic  39.6 us (6%)
  between operations  14.7 us (2%)
    psum x1, waiting for transfers between devices, shards(): shard_gu, shard_down = lax.psum((shard_gu, shard_down), 'rep')  148 us
    psum x1, waiting for transfers between devices, shards(): shard_attn = lax.psum(shard_attn, 'rep').astype(jnp.float32)  73.8 us
    dot_general x7, matrix products, matmul(): return jnp.dot(left, right, preferred_element_type=jnp.float32)  57.2 us
    dot_general x7, matrix products, right_product(): jnp.einsum('tf,ef->te', rows_grad, weight, preferred_element_type=jnp.flo...  44.6 us
    pallas_call x1, Pallas kernels, attend_back(): pl.pallas_call(attend_back_kernel, grid=(kvh,), out_shape=(jax.ShapeDtype...  43.3 us
    reduce_scatter x1, waiting for transfers between devices, shards(): lax.psum_scatter(pack_grad, 'grp', scatter_dimension=0, tiled=True)  43 us
    unnamed x87, local copies, waits for them, and re-layouts  38.9 us
    dot_general x7, matrix products, left_product(): jnp.einsum('te,tf->ef', rows_in, rows_grad, preferred_element_type=jnp.fl...  35.3 us
  transfers between devices with their start and end apart: 9, of which 6 were waited for; matrix products, arithmetic and copies ran while one was open for 27% of the time, Pallas kernels for 10%

profile of v2, /device:TPU:0, one launch (start us, length us, event | category | flops | bytes accessed | tf_op | source)
XLA Modules:
  0.0 700.7 jit_solution(12185684101583851737)
XLA Ops:
  11.8 3.5 concatenate.37
  20.0 30.8 %all-gather.11.cloned.1.call-done = bf16[2560,960]{0,1:T(8,128)(2,1)} async-done(((bf16[640,960]{0,1:T(8,128)(2,1)}), bf16[2560,960]{0,1:T(8,128)(2,1)}) %all-gather.11.cloned.1.call-update) | async-done | bytes 4915216 | tf_op jit(solution)/shard_map/all_gather | solution.py:226
  50.8 10.6 %fusion.39 = f32[1024,2560]{1,0:T(8,128)} fusion(bf16[1024,960]{0,1:T(8,128)(2,1)} %param.23, bf16[2560,960]{0,1:T(8,128)(2,1)} %all-gather.11.cloned.1.call-done), kind=kOutput, calls=%fused_computation.93 | convolution fusion | flops 5033164800 | bytes 17367040 | tf_op jit(solution)/shard_map/tf,ef->te/dot_general | solution.py:62
  61.4 31.6 %all-gather.5.cloned.1.call-done = bf16[960,2688]{1,0:T(8,128)(2,1)} async-done(((bf16[240,2688]{1,0:T(8,128)(2,1)}), bf16[960,2688]{1,0:T(8,128)(2,1)}) %all-gather.5.cloned.1.call-update) | async-done | bytes 5160976 | tf_op jit(solution)/shard_map/all_gather | solution.py:217
  94.4 2.7 fusion.24
  98.2 2.9 copy.106
  101.1 2.9 copy.107
  104.0 4.2 fusion.16
  110.3 4.7 copy.83
  115.0 4.5 copy.84
  119.5 2.9 convolution_convert_fusion.8
  122.4 2.1 copy.89
  124.5 3.4 subtract_convert_fusion.1
  130.1 2.2 maximum_bitcast_fusion.q_ref
  132.3 29.2 %attend.1 = (bf16[5,3,1024,64]{3,2,1,0:T(8,128)(2,1)S(1)}, f32[5,3,1024,1]{3,2,1,0:T(8,128)}) custom-call(bf16[5,3,1024,64]{3,2,1,0:T(8,128)(2,1)S(1)} %maximum_bitcast_fusion.q_ref, bf16[5,1024,64]{2,1,0:T(8,128)(2,1)S(1)} %maximum_bitcast_fusion.1.k_ref, bf16[5,1024,64]{2,1,0:T(8,128)(2,1)S(1)} %bitcast.61, s32[1024,1]{1,0:T(8,128)S(1)} %copy.90.col_ref, ...), custom_call_target="tpu_custom_call" | custom-call | flops 20000000000 | bytes 20000000 | tf_op jit(solution)/shard_map/attend/pallas_call | solution.py:151
  163.4 4.7 copy.91
  168.1 5.9 multiply_reduce_fusion.2
  177.7 10.7 %fusion.38 = f32[1024,2560]{1,0:T(8,128)} fusion(bf16[1024,960]{0,1:T(8,128)(2,1)} %multiply_convert_fusion.3, bf16[960,2560]{1,0:T(8,128)(2,1)} %all-gather.9.cloned.1.call-done), kind=kOutput, calls=%fused_computation.92 | convolution fusion | flops 5033164800 | bytes 17367040 | tf_op jit(solution)/shard_map/dot_general | solution.py:54
  188.4 20.1 %multiply_convert_fusion.1 = (bf16[1024,2560]{1,0:T(8,128)(2,1)}, bf16[1024,2560]{1,0:T(8,128)(2,1)}, bf16[1024,2560]{1,0:T(8,128)(2,1)}) fusion(f32[1024,2560]{1,0:T(8,128)} %fusion.39, f32[1024,2560]{1,0:T(8,128)} %fusion.38, bf16[1024,960]{0,1:T(8,128)(2,1)} %multiply_convert_fusion.3, bf16[960,2560]{1,0:T(8,128)(2,1)} %all-gather.7.cloned.1.call-done), kind=kOutput, calls=%fused_computation.1 | convolution fusion | flops 5072486400 | bytes 43581440 | tf_op jit(solution)/shard_map/dot_general | solution.py:54
  208.5 8.1 %convolution_convert_fusion.2 = bf16[960,2560]{1,0:T(8,128)(2,1)S(1)} fusion(bf16[1024,960]{0,1:T(8,128)(2,1)S(1)} %copy-done.23, bf16[1024,2560]{1,0:T(8,128)(2,1)} %get-tuple-element.87), kind=kOutput, calls=%fused_computation.13 | convolution fusion | flops 5035622400 | bytes 12124160 | tf_op jit(solution)/shard_map/te,tf->ef/dot_general | solution.py:58
  216.6 5.5 convolution_convert_fusion.1
  222.2 8.9 %fusion.40 = f32[1024,960]{0,1:T(8,128)} fusion(bf16[1024,2560]{1,0:T(8,128)(2,1)} %get-tuple-element.87, bf16[960,2560]{1,0:T(8,128)(2,1)S(1)} %bitcast.83), kind=kOutput, calls=%fused_computation.94 | convolution fusion | flops 5033164800 | bytes 14090240 | tf_op jit(solution)/shard_map/tf,ef->te/dot_general | solution.py:62
  231.1 9.6 %multiply_reduce_fusion = (bf16[960]{0:T(1024)(128)(2,1)S(1)}, f32[1024]{0:T(1024)S(1)}, f32[1024,960]{0,1:T(8,128)S(1)}) fusion(f32[1024,960]{0,1:T(8,128)S(1)} %copy-done.6, f32[1024]{0:T(1024)S(1)} %add_rsqrt_fusion, f32[960]{0:T(1024)S(1)} %get-tuple-element.81, f32[1024,960]{0,1:T(8,128)} %fusion.40, bf16[1024,2560]{1,0:T(8,128)(2,1)S(1)} %copy-done.33, ...), kind=kOutput, calls=%fused_computation.26 | convolution fusion | flops 5040044032 | bytes 21968512 | tf_op jit(solution)/shard_map/tf,ef->te/dot_general | solution.py:62
  240.7 9.4 %convolution_convert_fusion = bf16[2560,960]{0,1:T(8,128)(2,1)} fusion(bf16[1024,960]{0,1:T(8,128)(2,1)S(1)} %copy-done.20, bf16[1024,2560]{1,0:T(8,128)(2,1)} %get-tuple-element.89), kind=kOutput, calls=%fused_computation.11 | convolution fusion | flops 5035622400 | bytes 12124160 | tf_op jit(solution)/shard_map/te,tf->ef/dot_general | solution.py:58
  250.1 3.0 multiply_add_fusion
  253.1 4.6 pad_maximum_fusion
  257.6 7.9 %copy.104 = bf16[2560,960]{1,0:T(8,128)(2,1)} copy(bf16[2560,960]{0,1:T(8,128)(2,1)} %convolution_convert_fusion) | data formatting | bytes 9830400
  267.4 6.3 convolution_convert_fusion.3
  273.7 5.2 copy.92
  278.9 43.3 %attend_back.1 = (f32[5,3,1024,64]{3,2,1,0:T(8,128)}, f32[5,1024,64]{2,1,0:T(8,128)S(1)}, f32[5,1024,64]{2,1,0:T(8,128)}) custom-call(bf16[5,3,1024,64]{3,2,1,0:T(8,128)(2,1)} %copy-done, bf16[5,1024,64]{2,1,0:T(8,128)(2,1)S(1)} %maximum_bitcast_fusion.1.k_ref, bf16[5,1024,64]{2,1,0:T(8,128)(2,1)S(1)} %bitcast.62, bf16[5,3,1024,64]{3,2,1,0:T(8,128)(2,1)} %bitcast.67, ...), custom_call_target="tpu_custom_call" | custom-call | flops 49999998976 | bytes 30000000 | tf_op jit(solution)/shard_map/attend_back/pallas_call | solution.py:171
  325.1 16.0 %fusion.34 = (f32[1024,15,32]{2,0,1:T(8,128)}, f32[1024,15,32]{2,0,1:T(8,128)}) fusion(f32[1024,15,64]{2,0,1:T(8,128)} %bitcast.64), kind=kLoop, calls=%fused_computation.88 | loop fusion | bytes 7864320 | tf_op jit(solution)/shard_map/slice | solution.py:37
  341.1 5.6 copy.108
  346.7 6.0 copy.109
  356.1 2.3 subtract_convert_fusion.2
  358.7 3.2 fusion.22
  362.0 2.2 fusion.14
  364.2 3.8 fusion.11
  377.2 5.2 convolution_convert_fusion.5
  382.4 3.5 convolution_convert_fusion.4
  385.9 9.3 %concatenate.47 = bf16[960,2688]{1,0:T(8,128)(2,1)} concatenate(bf16[960,960]{1,0:T(8,128)(2,1)} %convolution_convert_fusion.5, bf16[960,320]{1,0:T(8,128)(2,1)S(1)} %copy.100, bf16[960,320]{1,0:T(8,128)(2,1)S(1)} %copy.101, bf16[960,960]{1,0:T(8,128)(2,1)} %convolution_convert_fusion.4, bf16[960,128]{1,0:T(8,128)(2,1)} %pad.10), dimensions={1} | concatenate | bytes 10321920 | tf_op jit(solution)/shard_map/concatenate | solution.py:303
  395.2 2.4 copy.105
  397.6 3.2 reduce-scatter.8.cloned.1.call-done
  400.9 10.5 %add_convert_fusion = bf16[1024,960]{0,1:T(8,128)(2,1)} fusion(f32[1024,960]{0,1:T(8,128)} %copy-done.5, bf16[1024,2560]{1,0:T(8,128)(2,1)} %get-tuple-element.89, bf16[2560,960]{0,1:T(8,128)(2,1)} %all-gather.11.cloned.1.call-done), kind=kOutput, calls=%fused_computation.30 | convolution fusion | flops 5035130880 | bytes 16056320 | tf_op jit(solution)/shard_map/dot_general | solution.py:54
  411.4 43.0 %reduce-scatter.6.cloned.1.call-done = bf16[240,2688]{1,0:T(8,128)(2,1)} async-done(((bf16[960,2688]{1,0:T(8,128)(2,1)}), bf16[240,2688]{1,0:T(8,128)(2,1)}) %reduce-scatter.6.cloned.1.call-update) | async-done | bytes 1290256 | tf_op jit(solution)/shard_map/reduce_scatter | solution.py:313
  454.4 148.0 %all-reduce.8.cloned.1.call-done = (bf16[240,5120]{1,0:T(8,128)(2,1)}, bf16[640,960]{0,1:T(8,128)(2,1)}) async-done(((bf16[240,5120]{1,0:T(8,128)(2,1)}, bf16[640,960]{0,1:T(8,128)(2,1)}), (bf16[240,5120]{1,0:T(8,128)(2,1)}, bf16[640,960]{0,1:T(8,128)(2,1)})) %all-reduce.8.cloned.1.call-update) | async-done | bytes 3686416 | tf_op jit(solution)/shard_map/psum | solution.py:273
  602.5 6.4 fusion.7
  611.5 2.9 slice_convert_fusion
  614.4 73.8 %all-reduce.6.cloned.1.call-done = bf16[240,2688]{1,0:T(8,128)(2,1)} async-done(((bf16[240,2688]{1,0:T(8,128)(2,1)}), bf16[240,2688]{1,0:T(8,128)(2,1)}) %all-reduce.6.cloned.1.call-update) | async-done | bytes 1290256 | tf_op jit(solution)/shard_map/psum | solution.py:315
  (151 shorter events, 47.6 us)
Async XLA Ops:
  7.2 43.7 %all-gather.11.cloned.1.call-start = ((), (), s32[]{:S(2)}) async-start(), calls=%async_computation.6 | async-start | bytes 6144000 | tf_op jit(solution)/shard_map/all_gather | solution.py:226
  7.9 8.8 %copy-start.3 = (bf16[1024,960]{0,1:T(8,128)(2,1)S(1)}, bf16[1024,960]{0,1:T(8,128)(2,1)}, u32[]{:S(2)}) copy-start(bf16[1024,960]{0,1:T(8,128)(2,1)} %param.12) | copy-start | bytes 5898244
  7.9 85.1 %all-gather.5.cloned.1.call-start = ((), (), s32[]{:S(2)}) async-start(), calls=%async_computation.3 | async-start | bytes 6451200 | tf_op jit(solution)/shard_map/all_gather | solution.py:217
  11.8 5.3 copy-start.2
  15.3 162.4 %all-gather.9.cloned.1.call-start = ((), (), s32[]{:S(2)}) async-start(), calls=%async_computation.5 | async-start | bytes 6144000 | tf_op jit(solution)/shard_map/all_gather | solution.py:225
  16.0 172.3 %all-gather.7.cloned.1.call-start = ((), (), s32[]{:S(2)}) async-start(), calls=%async_computation.4 | async-start | bytes 6144000 | tf_op jit(solution)/shard_map/all_gather | solution.py:224
  16.6 378.6 %reduce-scatter.10.cloned.1.call-start = ((), (), s32[]{:S(2)}) async-start(), calls=%async_computation.10 | async-start | bytes 6553600
  17.1 102.3 %copy-start.30 = (f32[1024]{0:T(1024)}, f32[1024]{0:T(1024)S(1)}, u32[]{:S(2)}) copy-start(f32[1024]{0:T(1024)S(1)} %add_rsqrt_fusion.1) | copy-start | bytes 12292
  19.1 0.7 copy-start.17
  19.1 0.7 copy-start.26
  19.3 105.2 %copy-start.11 = (f32[1024,32]{1,0:T(8,128)}, f32[1024,32]{1,0:T(8,128)S(1)}, u32[]{:S(2)}) copy-start(f32[1024,32]{1,0:T(8,128)S(1)} %copy.86) | copy-start | bytes 393220
  94.4 25.1 %copy-start.28 = (f32[960]{0:T(1024)}, f32[960]{0:T(1024)S(1)}, u32[]{:S(2)}) copy-start(f32[960]{0:T(1024)S(1)} %get-tuple-element.82) | copy-start | bytes 11524
  104.0 4.3 copy-start.18
  104.0 4.3 copy-start.27
  124.5 4.2 copy-start.9
  127.9 2.2 copy-start.8
  132.3 29.2 %copy-start = (bf16[5,3,1024,64]{3,2,1,0:T(8,128)(2,1)}, bf16[5,3,1024,64]{3,2,1,0:T(8,128)(2,1)S(1)}, u32[]{:S(2)}) copy-start(bf16[5,3,1024,64]{3,2,1,0:T(8,128)(2,1)S(1)} %maximum_bitcast_fusion.q_ref) | copy-start | bytes 5898244
  161.5 1.9 copy-start.1
  174.0 1.9 copy-start.5
  188.4 20.1 %copy-start.23 = (bf16[1024,960]{0,1:T(8,128)(2,1)S(1)}, bf16[1024,960]{0,1:T(8,128)(2,1)}, u32[]{:S(2)}) copy-start(bf16[1024,960]{0,1:T(8,128)(2,1)} %multiply_convert_fusion.3) | copy-start | bytes 5898244
  208.5 8.1 %copy-start.32 = (bf16[1024,2560]{1,0:T(8,128)(2,1)S(1)}, bf16[1024,2560]{1,0:T(8,128)(2,1)}, u32[]{:S(2)}) copy-start(bf16[1024,2560]{1,0:T(8,128)(2,1)} %get-tuple-element.88) | copy-start | bytes 15728644
  208.5 13.6 %slice-start.2 = ((s8[4915200]{0:T(1024)(128)(4,1)}), s8[4194304]{0:T(1024)(128)(4,1)S(1)}, s32[]{:S(2)}) async-start(s8[4915200]{0:T(1024)(128)(4,1)} %bitcast.82), calls=%async_computation.14 | async-start | bytes 8388608
  216.6 5.5 slice-start.3
  222.1 8.9 %copy-start.6 = (f32[1024,960]{0,1:T(8,128)S(1)}, f32[1024,960]{0,1:T(8,128)}, u32[]{:S(2)}) copy-start(f32[1024,960]{0,1:T(8,128)} %copy-done.5) | copy-start | bytes 11796484
  222.1 8.9 %copy-start.33 = (bf16[1024,2560]{1,0:T(8,128)(2,1)S(1)}, bf16[1024,2560]{1,0:T(8,128)(2,1)}, u32[]{:S(2)}) copy-start(bf16[1024,2560]{1,0:T(8,128)(2,1)} %get-tuple-element.88) | copy-start | bytes 15728644
  231.1 9.6 %copy-start.20 = (bf16[1024,960]{0,1:T(8,128)(2,1)S(1)}, bf16[1024,960]{0,1:T(8,128)(2,1)}, u32[]{:S(2)}) copy-start(bf16[1024,960]{0,1:T(8,128)(2,1)} %param.23) | copy-start | bytes 5898244
  265.5 0.9 copy-start.25
  265.5 135.3 %reduce-scatter.8.cloned.1.call-start = ((), (), s32[]{:S(2)}) async-start(), calls=%async_computation.8 | async-start | bytes 12288000 | tf_op jit(solution)/shard_map/reduce_scatter | solution.py:271
  266.1 188.3 %reduce-scatter.6.cloned.1.call-start = ((), (), s32[]{:S(2)}) async-start(), calls=%async_computation.7 | async-start | bytes 6451200 | tf_op jit(solution)/shard_map/reduce_scatter | solution.py:313
  278.9 43.3 %copy-start.12 = (f32[1024,32]{1,0:T(8,128)S(1)}, f32[1024,32]{1,0:T(8,128)}, u32[]{:S(2)}) copy-start(f32[1024,32]{1,0:T(8,128)} %copy-done.11) | copy-start | bytes 393220
  278.9 43.3 %copy-start.16 = (f32[1024,32]{1,0:T(8,128)S(1)}, f32[1024,32]{1,0:T(8,128)}, u32[]{:S(2)}) copy-start(f32[1024,32]{1,0:T(8,128)} %copy.96) | copy-start | bytes 393220
  352.7 3.4 copy-start.19
  356.1 2.6 copy-start.13
  356.1 5.8 slice-start
  358.5 3.5 slice-start.1
  358.7 3.2 copy-start.22
  361.9 2.2 copy-start.4
  361.9 2.2 copy-start.14
  362.0 2.2 copy-start.29
  362.0 2.2 copy-start.31
  377.1 5.2 copy-start.7
  377.1 5.2 copy-start.21
  395.2 207.3 %all-reduce.8.cloned.1.call-start = ((), (), s32[]{:S(2)}) async-start(), calls=%async_computation.11 | async-start | bytes 7372800 | tf_op jit(solution)/shard_map/psum | solution.py:273
  400.8 287.4 %all-reduce.6.cloned.1.call-start = ((), (), s32[]{:S(2)}) async-start(), calls=%async_computation.9 | async-start | bytes 2580480 | tf_op jit(solution)/shard_map/psum | solution.py:315
  602.5 6.4 copy-start.24
  608.9 2.6 copy-start.15
  688.2 2.4 copy-start.10
Sparse Core Ops, SparseCore 0:
  9.6 41.2 all-gather.10
  53.0 39.9 all-gather.4
  94.6 38.5 all-gather.8
  134.6 38.5 all-gather.6
  265.6 51.4 reduce-scatter.9
  319.8 81.0 reduce-scatter.7
  403.6 50.8 reduce-scatter.5
  458.7 143.7 all-reduce.7
  606.1 82.0 all-reduce.5
